TPU v7x, 1024 devices: a whole 4x8x16 slice. The times are simulated.
1024 devices in a mesh: row: 32 (over y_lo, x, core), col: 32 (over y_hi, z).
Axes of the slice: x: 4, y: 8 (y_hi: 2, y_lo: 4; y = y_hi * 4 + y_lo), z: 16, core: 2. Of those that a mesh axis runs over, the one named last changes fastest.
Arguments:
- left_term: bfloat16 [32, 32, 1, 2, 128, 128], P('row', 'col'), may hold values from -6 to 6
- right_factor: bfloat16 [32, 32, 128, 256], P('row', 'col'), may hold values from -0.75 to 0.75
- targets: int32 [32, 32, 32, 1], P('row', 'col'), may hold values from 0 to 8, as said below
- propagator_in: float32 [32, 32, 8, 2, 128, 128], P('row', 'col'), may hold values from -6 to 6
Outputs:
- next_term: bfloat16 [32, 32, 8, 2, 128, 128], P('row', 'col')
- propagator: float32 [32, 32, 8, 2, 128, 128], P('row', 'col')
Inputs may be any that keep to these rules, and one draw needn't show every extreme that they name: `targets`: an entry equal to 8 means the block product is filtered out. On each device the share of entries below 8 is exactly 1/16, 1/8, 1/4 or 1/2.
All inputs are finite; a program needn't handle non-finite values.
Results may differ from a plain program's by a relative error of at most 0.001.
Values may be sent and summed in bfloat16 or wider, within the bound.
No kernel may reach another device: no remote copies, remote signals or barrier semaphores. Data moves between devices by JAX's collectives and lax.ppermute only.
A program may use at most 32 MiB of HBM per device.

v0:
```python
import jax
import jax.numpy as jnp
from jax import lax
from jax.sharding import PartitionSpec as P

ORDER = 2


STEP_SIZE = 0.5


def per_device(left_term, right_factor, targets, propagator_in):
    grid_rows = lax.axis_size("row")
    edge = left_term.shape[4]
    slot_count = propagator_in.shape[2]
    local_targets = targets[0, 0]
    scaling = STEP_SIZE / ORDER
    whole_panel = lax.all_gather(left_term, "col", axis=1, tiled=True)[0]

    def left_for(panel_index):
        return lax.dynamic_index_in_dim(whole_panel, panel_index, 0, keepdims=False)

    def contribution(lefts, right_block):
        member_total = lefts.shape[0]
        products = jnp.dot(
            lefts.reshape(member_total * 2 * edge, edge),
            right_block,
            preferred_element_type=jnp.float32,
        )
        products = products.reshape(member_total, 2, edge, 2, edge)
        real_part = products[:, 0, :, 0] - products[:, 1, :, 1]
        imag_part = products[:, 0, :, 1] + products[:, 1, :, 0]
        return jnp.stack([scaling * imag_part, -scaling * real_part], axis=1)

    def add_into(totals, update, target_slot):
        active = target_slot < slot_count
        clipped_slot = jnp.minimum(target_slot, slot_count - 1)
        previous = lax.dynamic_index_in_dim(totals, clipped_slot, 0, keepdims=False)
        return lax.dynamic_update_index_in_dim(
            totals, previous + jnp.where(active, update, 0.0), clipped_slot, 0
        )

    def accumulate(totals, lefts, right_block, panel_index):
        wanted = lax.dynamic_index_in_dim(local_targets, panel_index, 0, keepdims=False)
        pieces = contribution(lefts, right_block)
        totals = add_into(totals, pieces[0], wanted[0])
        return totals

    start_totals = jnp.zeros((slot_count, 2, edge, edge), jnp.float32)
    whole_right = lax.all_gather(right_factor, "row", axis=0, tiled=True)[:, 0]

    def gathered_advance(position, totals):
        right_block = lax.dynamic_index_in_dim(whole_right, position, 0, keepdims=False)
        return accumulate(totals, left_for(position), right_block, position)

    totals = lax.fori_loop(0, grid_rows, gathered_advance, start_totals)
    next_full = totals[None, None]
    return (next_full.astype(jnp.bfloat16), propagator_in + next_full)


def solution(mesh):
    in_specs = (
        P("row", "col", None, None, None, None),
        P("row", "col", None, None),
        P("row", "col", None, None),
        P("row", "col", None, None, None, None),
    )
    out_specs = (P("row", "col", None, None, None, None), P("row", "col", None, None, None, None))
    return jax.shard_map(
        per_device, mesh=mesh, in_specs=in_specs, out_specs=out_specs, check_vma=False
    )
```

profile of v0, /device:TPU:1, one launch (start us, length us, event | category | flops | bytes accessed | tf_op | source)
XLA Modules:
  0.0 449.6 jit_solution(8883811561323048739)
XLA Ops:
  8.6 168.3 %all-gather.3.cloned.1.call-done = bf16[1,32,1,2,128,128]{5,4,3,2,0,1:T(8,128)(2,1)} async-done(((bf16[1,1,1,2,128,128]{5,4,3,2,0,1:T(8,128)(2,1)}), bf16[1,32,1,2,128,128]{5,4,3,2,0,1:T(8,128)(2,1)}) %all-gather.3.cloned.1.call-update) | async-done | bytes 2097168 | tf_op jit(solution)/shard_map/all_gather | solution.py:18
  177.0 76.7 %all-gather.5.cloned.1.call-done = bf16[32,1,128,256]{3,2,1,0:T(8,128)(2,1)} async-done(((bf16[1,1,128,256]{3,2,1,0:T(8,128)(2,1)}), bf16[32,1,128,256]{3,2,1,0:T(8,128)(2,1)}) %all-gather.5.cloned.1.call-update) | async-done | bytes 2097168 | tf_op jit(solution)/shard_map/all_gather | solution.py:50
  253.8 186.5 %while.13 = (s32[]{:T(128)}, f32[8,2,128,128]{3,2,1,0:T(8,128)S(1)}, s32[32,1]{0,1:T(1,128)}, bf16[32,1,2,128,128]{4,3,2,1,0:T(8,128)(2,1)}, bf16[32,128,256]{2,...) while((s32[]{:T(128)}, f32[8,2,128,128]{3,2,1,0:T(8,128)S(1)}, ...), condition=%wide.region_1.2_spmd, body=%wide.region_0.1_spmd.sunk | while | flops 16941060 | bytes 1441965 | solution.py:56
  253.8 1.2 fusion.18
  259.6 1.2 fusion.18
  265.4 1.2 fusion.18
  271.3 1.2 fusion.18
  277.1 1.2 fusion.18
  282.9 1.2 fusion.18
  288.8 1.2 fusion.18
  294.6 1.2 fusion.18
  300.4 1.2 fusion.18
  306.2 1.2 fusion.18
  312.1 1.2 fusion.18
  317.9 1.2 fusion.18
  323.7 1.2 fusion.18
  329.5 1.2 fusion.18
  335.4 1.2 fusion.18
  341.2 1.2 fusion.18
  347.0 1.2 fusion.18
  352.9 1.2 fusion.18
  358.7 1.2 fusion.18
  364.5 1.2 fusion.18
  370.3 1.2 fusion.18
  376.2 1.2 fusion.18
  382.0 1.2 fusion.18
  387.8 1.2 fusion.18
  393.6 1.2 fusion.18
  399.5 1.2 fusion.18
  405.3 1.2 fusion.18
  411.1 1.2 fusion.18
  417.0 1.2 fusion.18
  (172 shorter events, 72.9 us)
Async XLA Ops:
  7.2 169.8 %all-gather.3.cloned.1.call-start = ((), (), s32[]{:S(2)}) async-start(), calls=%async_computation | async-start | bytes 2162688 | tf_op jit(solution)/shard_map/all_gather | solution.py:18
  7.9 245.8 %all-gather.5.cloned.1.call-start = ((), (), s32[]{:S(2)}) async-start(), calls=%async_computation.1 | async-start | bytes 2162688 | tf_op jit(solution)/shard_map/all_gather | solution.py:50
  440.3 1.4 copy-start
Sparse Core Ops, SparseCore 0:
  12.3 164.6 all-gather.2
  179.7 73.9 all-gather.4
where the time goes:
time: 454 us; the launch traced here: 450 us
  waiting for transfers between devices  246 us (54%)
  loops' own time  81.5 us (18%)
  other arithmetic  43.3 us (10%)
  matrix products  32.8 us (7%)
  local copies, waits for them, and re-layouts  31.4 us (7%)
  between operations  14.1 us (3%)
    all_gather x1, waiting for transfers between devices, per_device(): whole_panel = lax.all_gather(left_term, 'col', axis=1, tiled=True)[0]  168 us
    another operation x1, loops' own time, per_device(): totals = lax.fori_loop(0, grid_rows, gathered_advance, start_totals)  81.5 us
    all_gather x1, waiting for transfers between devices, per_device(): whole_right = lax.all_gather(right_factor, 'row', axis=0, tiled=True)[:, 0]  76.7 us
    min x32, other arithmetic, add_into(): clipped_slot = jnp.minimum(target_slot, slot_count - 1)  39.8 us
    dot_general x32, matrix products, contribution(): jnp.dot(lefts.reshape(member_total * 2 * edge, edge), right_block, prefer...  32.8 us
    dynamic_slice x64, local copies, waits for them, and re-layouts, gathered_advance(): lax.dynamic_index_in_dim(whole_right, position, 0, keepdims=False)  30.8 us
  transfers between devices with their start and end apart: 2, of which 2 were waited for; matrix products, arithmetic and copies ran while one was open for 0% of the time, Pallas kernels for 0%

commit v1 on v0

v1 whole, which is shorter than its diff:
```python
import jax
import jax.numpy as jnp
from jax import lax
from jax.experimental import pallas as pl
from jax.experimental.pallas import tpu as pltpu
from jax.sharding import PartitionSpec as P

ORDER = 2
STEP_SIZE = 0.5
SCALING = STEP_SIZE / ORDER
RUNS = 2
CLASSES = 4


def shifted(columns, step):
    length = columns // RUNS
    return [
        (run * length + place, run * length + (place + step) % length)
        for run in range(RUNS)
        for place in range(length)
    ]


def gather_left(pair, columns):
    length = columns // RUNS
    groups = [
        [run * length + member * CLASSES + start for member in range(length // CLASSES)]
        for run in range(RUNS)
        for start in range(CLASSES)
    ]
    own = lax.all_gather(pair, "col", axis_index_groups=groups)
    half = own.shape[0] // 2
    after = lax.ppermute(own, "col", shifted(columns, -1))
    before = lax.ppermute(own, "col", shifted(columns, 1))
    far_low = lax.ppermute(own[:half], "col", shifted(columns, 2))
    far_high = lax.ppermute(own[half:], "col", shifted(columns, -2))
    return own, after, far_low, far_high, before


def product_kernel(
    members, place_ref, targets_ref, own, after, far_low, far_high, before, right, base_ref,
    next_hbm, sum_hbm, totals, next_buf, sum_buf, next_sem, sum_sem,
):
    slots = totals.shape[0]
    edge = totals.shape[2]
    length = members * CLASSES
    start, my_run = place_ref[0], place_ref[1]
    totals[...] = jnp.zeros_like(totals)

    def add_class(ref, distance, first, count):
        residue = lax.rem(start + distance, CLASSES)

        def step(index, carry):
            member = first + index // RUNS
            flip = lax.rem(index, RUNS)
            run = lax.rem(my_run + flip, RUNS)
            panel = run * length + member * CLASSES + residue
            slot = targets_ref[panel]

            @pl.when(slot < slots)
            def _():
                product = jnp.dot(
                    ref[index // RUNS, flip], right[panel], preferred_element_type=jnp.float32
                )
                real = product[:edge, :edge] - product[edge:, edge:]
                imag = product[:edge, edge:] + product[edge:, :edge]
                totals[slot, 0] += imag
                totals[slot, 1] -= real

            return carry

        lax.fori_loop(0, count * RUNS, step, 0)

    add_class(own, 0, 0, members)
    add_class(after, 1, 0, members)
    add_class(far_low, 2, 0, members // 2)
    add_class(far_high, 2, members // 2, members // 2)
    add_class(before, 3, 0, members)

    def out_copies(slot):
        return (
            pltpu.make_async_copy(next_buf.at[slot], next_hbm.at[slot], next_sem.at[slot]),
            pltpu.make_async_copy(sum_buf.at[slot], sum_hbm.at[slot], sum_sem.at[slot]),
        )

    for slot in range(slots):
        term = totals[slot] * SCALING
        next_buf[slot] = term.astype(jnp.bfloat16)
        sum_buf[slot] = base_ref[slot] + term
        for copy in out_copies(slot):
            copy.start()
    for slot in range(slots):
        for copy in out_copies(slot):
            copy.wait()


def per_device(left_term, right_factor, targets, propagator_in):
    columns, rows = lax.axis_size("col"), lax.axis_size("row")
    edge = left_term.shape[4]
    slots = propagator_in.shape[2]
    length = columns // RUNS
    members = length // CLASSES
    mine = left_term.reshape(2 * edge, edge)
    other = lax.ppermute(
        mine, "col", [(c, (c + length) % columns) for c in range(columns)]
    )
    pair = jnp.stack([mine, other])
    copies = jnp.broadcast_to(right_factor[0, 0], (rows, edge, 2 * edge))
    pair, copies = lax.optimization_barrier((pair, copies))
    right = lax.all_to_all(copies, "row", 0, 0)
    own, after, far_low, far_high, before = gather_left(pair, columns)
    column = lax.axis_index("col")
    place = jnp.stack([column % CLASSES, column // length]).astype(jnp.int32)
    block = (slots, 2, edge, edge)
    in_vmem = pl.BlockSpec(memory_space=pltpu.VMEM)
    in_smem = pl.BlockSpec(memory_space=pltpu.SMEM)
    in_any = pl.BlockSpec(memory_space=pl.ANY)

    def kernel(*refs):
        product_kernel(members, *refs)

    next_term, total = pl.pallas_call(
        kernel,
        out_shape=(
            jax.ShapeDtypeStruct(block, jnp.bfloat16),
            jax.ShapeDtypeStruct(block, jnp.float32),
        ),
        in_specs=[in_smem, in_smem] + [in_vmem] * 7,
        out_specs=(in_any, in_any),
        scratch_shapes=[
            pltpu.VMEM(block, jnp.float32),
            pltpu.VMEM(block, jnp.bfloat16),
            pltpu.VMEM(block, jnp.float32),
            pltpu.SemaphoreType.DMA((slots,)),
            pltpu.SemaphoreType.DMA((slots,)),
        ],
        compiler_params=pltpu.CompilerParams(vmem_limit_bytes=24 * 1024 * 1024),
        cost_estimate=pl.CostEstimate(flops=300_000_000, bytes_accessed=7_000_000, transcendentals=0),
    )(
        place, targets[0, 0, :, 0], own, after, far_low, far_high, before, right,
        propagator_in.reshape(block),
    )
    shape = propagator_in.shape
    return next_term.reshape(shape), total.reshape(shape)


def solution(mesh):
    in_specs = (
        P("row", "col", None, None, None, None),
        P("row", "col", None, None),
        P("row", "col", None, None),
        P("row", "col", None, None, None, None),
    )
    out_specs = (P("row", "col", None, None, None, None), P("row", "col", None, None, None, None))
    return jax.shard_map(
        per_device, mesh=mesh, in_specs=in_specs, out_specs=out_specs, check_vma=False
    )
```

time: 454 us -> 102 us (0.22)
  the two profiles are of different devices: /device:TPU:1 before, /device:TPU:62 now
where the time goes in v1:
time: 102 us
  starting transfers between devices  37.7 us (37%)
  blocking collectives  31.8 us (31%)
  waiting for transfers between devices  20.4 us (20%)
  Pallas kernels  5.81 us (6%)
  local copies, waits for them, and re-layouts  4.46 us (4%)
    all_gather x1, blocking collectives, gather_left(): own = lax.all_gather(pair, 'col', axis_index_groups=groups)  31.8 us
    ppermute x1, waiting for transfers between devices, gather_left(): far_low = lax.ppermute(own[:half], 'col', shifted(columns, 2))  13.7 us
    all_to_all x1, starting transfers between devices, per_device(): right = lax.all_to_all(copies, 'row', 0, 0)  12.7 us
    ppermute x1, starting transfers between devices, gather_left(): after = lax.ppermute(own, 'col', shifted(columns, -1))  7.67 us
    ppermute x1, waiting for transfers between devices, per_device(): lax.ppermute(mine, 'col', [(c, (c + length) % columns) for c in range(col...  6.53 us
    ppermute x1, starting transfers between devices, gather_left(): far_high = lax.ppermute(own[half:], 'col', shifted(columns, -2))  6.03 us
    pallas_call x1, Pallas kernels, per_device(): pl.pallas_call(kernel, out_shape=(jax.ShapeDtypeStruct(block, jnp.bfloat1...  5.81 us
    ppermute x1, starting transfers between devices, per_device(): lax.ppermute(mine, 'col', [(c, (c + length) % columns) for c in range(col...  4.71 us
  transfers between devices with their start and end apart: 6, of which 3 were waited for; matrix products, arithmetic and copies ran while one was open for 1% of the time, Pallas kernels for 0%

profile of v1, /device:TPU:62, one launch (start us, length us, event | category | flops | bytes accessed | tf_op | source)
XLA Modules:
  0.0 101.8 jit_solution(195840341678146376)
XLA Ops:
  0.6 4.7 %collective-permute-start = (bf16[256,128]{1,0:T(8,128)(2,1)}, bf16[256,128]{1,0:T(8,128)(2,1)S(1)}, u32[]{:S(2)}, u32[]{:S(2)}) collective-permute-start(bf16[256,128]{1,0:T(8,128)(2,1)} %bitcast.19), channel_id=1, source_target_pairs={{0,16},{1,17},{2,18},{3,19},{4,20},{5,21},{6,22},{7,23},{8,24},{9,... | collective-permute-start | bytes 196616 | tf_op jit(solution)/shard_map/ppermute | solution.py:104
  5.3 6.5 %collective-permute-done = bf16[256,128]{1,0:T(8,128)(2,1)S(1)} collective-permute-done((bf16[256,128]{1,0:T(8,128)(2,1)}, bf16[256,128]{1,0:T(8,128)(2,1)S(1)}, u32[]{:S(2)}, u32[]{:S(2)}) %collective-permute-start) | collective-permute-done | bytes 65568 | tf_op jit(solution)/shard_map/ppermute | solution.py:104
  11.9 0.9 pad_maximum_fusion
  12.7 2.4 %broadcast_in_dim.3 = bf16[32,128,256]{2,1,0:T(8,128)(2,1)} broadcast(bf16[128,256]{1,0:T(8,128)(2,1)} %bitcast.18), dimensions={1,2} | broadcast | bytes 2162688 | tf_op jit(solution)/shard_map/broadcast_in_dim | solution.py:108
  15.1 0.0 copy-start.1
  15.1 12.7 %all-to-all-start = ((bf16[32,128,256]{2,1,0:T(8,128)(2,1)}), bf16[32,128,256]{2,1,0:T(8,128)(2,1)S(1)}, u32[]{:S(2)}, u32[]{:S(2)}) async-start(bf16[32,128,256]{2,1,0:T(8,128)(2,1)} %broadcast_in_dim.3), calls=%async_computation | async-start | bytes 4194304 | tf_op jit(solution)/shard_map/all_to_all | solution.py:110
  27.8 31.8 %all-gather = bf16[8,256,128]{2,1,0:T(8,128)(2,1)S(1)} all-gather(bf16[2,256,128]{2,1,0:T(8,128)(2,1)S(1)} %pad_maximum_fusion), channel_id=2, replica_groups={{0,4,8,12},{1,5,9,13},{2,6,10,14},{3,7,11,15},{16,20,24,28},{17,21,25,2..., dimensions={0}, use_global_device_ids=true | all-gather | bytes 655360 | tf_op jit(solution)/shard_map/all_gather | solution.py:31
  59.7 4.7 %collective-permute-start.4 = (bf16[4,2,256,128]{3,2,1,0:T(8,128)(2,1)S(1)}, bf16[4,2,256,128]{3,2,1,0:T(8,128)(2,1)S(1)}, u32[]{:S(2)}, u32[]{:S(2)}) collective-permute-start(bf16[4,2,256,128]{3,2,1,0:T(8,128)(2,1)S(1)} %bitcast.13), channel_id=1, source_target_pairs={{0,1},{1,2},{2,3},{3,4},{4,5},{5,6},{6,7},{7,8},{8,9},{9,10},{10,1... | collective-permute-start | bytes 1572872 | tf_op jit(solution)/shard_map/ppermute | solution.py:34
  64.3 7.7 %collective-permute-start.1 = (bf16[4,2,256,128]{3,2,1,0:T(8,128)(2,1)S(1)}, bf16[4,2,256,128]{3,2,1,0:T(8,128)(2,1)}, u32[]{:S(2)}, u32[]{:S(2)}) collective-permute-start(bf16[4,2,256,128]{3,2,1,0:T(8,128)(2,1)S(1)} %bitcast.14), channel_id=1, source_target_pairs={{0,15},{1,0},{2,1},{3,2},{4,3},{5,4},{6,5},{7,6},{8,7},{9,8},{10,9... | collective-permute-start | bytes 1572872 | tf_op jit(solution)/shard_map/ppermute | solution.py:33
  72.0 0.8 fusion
  72.9 1.9 %collective-permute-start.2 = (bf16[2,2,256,128]{3,2,1,0:T(8,128)(2,1)}, bf16[2,2,256,128]{3,2,1,0:T(8,128)(2,1)S(1)}, u32[]{:S(2)}, u32[]{:S(2)}) collective-permute-start(bf16[2,2,256,128]{3,2,1,0:T(8,128)(2,1)} %bitcast.8), channel_id=1, source_target_pairs={{0,2},{1,3},{2,4},{3,5},{4,6},{5,7},{6,8},{7,9},{8,10},{9,11},{10,... | collective-permute-start | bytes 786440 | tf_op jit(solution)/shard_map/ppermute | solution.py:35
  74.8 6.0 %collective-permute-start.3 = (bf16[2,2,256,128]{3,2,1,0:T(8,128)(2,1)}, bf16[2,2,256,128]{3,2,1,0:T(8,128)(2,1)}, u32[]{:S(2)}, u32[]{:S(2)}) collective-permute-start(bf16[2,2,256,128]{3,2,1,0:T(8,128)(2,1)} %bitcast.9), channel_id=1, source_target_pairs={{0,14},{1,15},{2,0},{3,1},{4,2},{5,3},{6,4},{7,5},{8,6},{9,7},{10,... | collective-permute-start | bytes 786440 | tf_op jit(solution)/shard_map/ppermute | solution.py:36
  80.8 0.1 pad_add_fusion.refs_0_
  80.9 13.7 %collective-permute-done.2.refs_4_ = bf16[2,2,256,128]{3,2,1,0:T(8,128)(2,1)S(1)} collective-permute-done((bf16[2,2,256,128]{3,2,1,0:T(8,128)(2,1)}, bf16[2,2,256,128]{3,2,1,0:T(8,128)(2,1)S(1)}, u32[]{:S(2)}, u32[]{:S(2)}) %collective-permute-start.2) | collective-permute-done | bytes 262176 | tf_op jit(solution)/shard_map/ppermute | solution.py:35
  94.6 0.1 collective-permute-done.3.refs_5_
  94.7 0.0 collective-permute-done.4.refs_6_
  94.7 0.0 collective-permute-done.1.refs_3_
  94.7 0.0 all-to-all-done.refs_7_
  94.7 0.0 copy-done.1
  94.7 0.0 copy-start
  94.8 1.2 %copy-done = f32[1,1,8,2,128,128]{5,4,3,2,1,0:T(8,128)S(1)} copy-done((f32[1,1,8,2,128,128]{5,4,3,2,1,0:T(8,128)S(1)}, f32[1,1,8,2,128,128]{5,4,3,2,1,0:T(8,128)}, u32[]{:S(2)}) %copy-start) | copy-done | bytes 1048600
  96.0 5.8 %shard_map.59 = (bf16[8,2,128,128]{3,2,1,0:T(8,128)(2,1)}, f32[8,2,128,128]{3,2,1,0:T(8,128)}) custom-call(s32[2]{0:T(128)S(1)} %pad_add_fusion.refs_0_, s32[32]{0:T(128)S(1)} %bitcast.17, bf16[4,2,256,128]{3,2,1,0:T(8,128)(2,1)S(1)} %bitcast.15, bf16[4,2,256,128]{3,2,1,0:T(8,128)(2,1)} %collective-permute-done.1.refs_3_, ...), custom_call_target="tpu_custom_call" | custom-call | flops 300000000 | bytes 7000000 | tf_op jit(solution)/shard_map/pallas_call | solution.py:122
Async XLA Ops:
  0.6 11.2 %collective-permute-start = (bf16[256,128]{1,0:T(8,128)(2,1)}, bf16[256,128]{1,0:T(8,128)(2,1)S(1)}, u32[]{:S(2)}, u32[]{:S(2)}) collective-permute-start(bf16[256,128]{1,0:T(8,128)(2,1)} %bitcast.19), channel_id=1, source_target_pairs={{0,16},{1,17},{2,18},{3,19},{4,20},{5,21},{6,22},{7,23},{8,24},{9,... | collective-permute-start | bytes 196616 | tf_op jit(solution)/shard_map/ppermute | solution.py:104
  15.1 79.6 %copy-start.1 = (s32[1,1,32,1]{2,3,1,0:T(1,128)S(1)}, s32[1,1,32,1]{2,3,1,0:T(1,128)}, u32[]{:S(2)}) copy-start(s32[1,1,32,1]{2,3,1,0:T(1,128)} %param.6) | copy-start | bytes 388
  15.1 79.6 %all-to-all-start = ((bf16[32,128,256]{2,1,0:T(8,128)(2,1)}), bf16[32,128,256]{2,1,0:T(8,128)(2,1)S(1)}, u32[]{:S(2)}, u32[]{:S(2)}) async-start(bf16[32,128,256]{2,1,0:T(8,128)(2,1)} %broadcast_in_dim.3), calls=%async_computation | async-start | bytes 4194304 | tf_op jit(solution)/shard_map/all_to_all | solution.py:110
  59.7 35.1 %collective-permute-start.4 = (bf16[4,2,256,128]{3,2,1,0:T(8,128)(2,1)S(1)}, bf16[4,2,256,128]{3,2,1,0:T(8,128)(2,1)S(1)}, u32[]{:S(2)}, u32[]{:S(2)}) collective-permute-start(bf16[4,2,256,128]{3,2,1,0:T(8,128)(2,1)S(1)} %bitcast.13), channel_id=1, source_target_pairs={{0,1},{1,2},{2,3},{3,4},{4,5},{5,6},{6,7},{7,8},{8,9},{9,10},{10,1... | collective-permute-start | bytes 1572872 | tf_op jit(solution)/shard_map/ppermute | solution.py:34
  64.3 30.4 %collective-permute-start.1 = (bf16[4,2,256,128]{3,2,1,0:T(8,128)(2,1)S(1)}, bf16[4,2,256,128]{3,2,1,0:T(8,128)(2,1)}, u32[]{:S(2)}, u32[]{:S(2)}) collective-permute-start(bf16[4,2,256,128]{3,2,1,0:T(8,128)(2,1)S(1)} %bitcast.14), channel_id=1, source_target_pairs={{0,15},{1,0},{2,1},{3,2},{4,3},{5,4},{6,5},{7,6},{8,7},{9,8},{10,9... | collective-permute-start | bytes 1572872 | tf_op jit(solution)/shard_map/ppermute | solution.py:33
  72.9 21.8 %collective-permute-start.2 = (bf16[2,2,256,128]{3,2,1,0:T(8,128)(2,1)}, bf16[2,2,256,128]{3,2,1,0:T(8,128)(2,1)S(1)}, u32[]{:S(2)}, u32[]{:S(2)}) collective-permute-start(bf16[2,2,256,128]{3,2,1,0:T(8,128)(2,1)} %bitcast.8), channel_id=1, source_target_pairs={{0,2},{1,3},{2,4},{3,5},{4,6},{5,7},{6,8},{7,9},{8,10},{9,11},{10,... | collective-permute-start | bytes 786440 | tf_op jit(solution)/shard_map/ppermute | solution.py:35
  74.8 20.0 %collective-permute-start.3 = (bf16[2,2,256,128]{3,2,1,0:T(8,128)(2,1)}, bf16[2,2,256,128]{3,2,1,0:T(8,128)(2,1)}, u32[]{:S(2)}, u32[]{:S(2)}) collective-permute-start(bf16[2,2,256,128]{3,2,1,0:T(8,128)(2,1)} %bitcast.9), channel_id=1, source_target_pairs={{0,14},{1,15},{2,0},{3,1},{4,2},{5,3},{6,4},{7,5},{8,6},{9,7},{10,... | collective-permute-start | bytes 786440 | tf_op jit(solution)/shard_map/ppermute | solution.py:36
  94.7 1.2 %copy-start = (f32[1,1,8,2,128,128]{5,4,3,2,1,0:T(8,128)S(1)}, f32[1,1,8,2,128,128]{5,4,3,2,1,0:T(8,128)}, u32[]{:S(2)}) copy-start(f32[1,1,8,2,128,128]{5,4,3,2,1,0:T(8,128)} %param.7) | copy-start | bytes 3145732

commit v2 on v1

v2 whole, which is shorter than its diff:
```python
import jax
import jax.numpy as jnp
from jax import lax
from jax.experimental import pallas as pl
from jax.experimental.pallas import tpu as pltpu
from jax.sharding import PartitionSpec as P

ORDER = 2
STEP_SIZE = 0.5
SCALING = STEP_SIZE / ORDER
RUNS = 2
CORES = 2
STRIDE = 4


def moved(value, columns, step):
    length = columns // RUNS
    pairs = [
        (run * length + place, run * length + (place + step) % length)
        for run in range(RUNS)
        for place in range(length)
    ]
    return lax.ppermute(value, "col", pairs)


def spread_kernel(block, copies, sems):
    moves = [pltpu.make_async_copy(block, copies.at[to], sems.at[to]) for to in range(copies.shape[0])]
    for move in moves:
        move.start()
    for move in moves:
        move.wait()


def add_panels(layout, length, meta, lefts, same_core, other_core, totals):
    slots, edge = totals.shape[0], totals.shape[2]
    panels = RUNS * length
    place, my_run, my_core = meta[panels], meta[panels + 1], meta[panels + 2]
    for ref, (delta, first) in zip(lefts, layout, strict=True):
        start = lax.rem(place + (delta + length), STRIDE)

        def step(index, carry, ref=ref, start=start, first=first):
            member, flip = index // RUNS, lax.rem(index, RUNS)
            run = lax.rem(my_run + flip, RUNS)
            panel = run * length + (first + member) * STRIDE + start
            slot = meta[panel]

            @pl.when(slot < slots)
            def _():
                at = panel // CORES
                block = jnp.where(panel % CORES == my_core, same_core[at], other_core[at])
                product = jnp.dot(ref[member, flip], block, preferred_element_type=jnp.float32)
                totals[slot, 0] += product[:edge, edge:] + product[edge:, :edge]
                totals[slot, 1] += product[edge:, edge:] - product[:edge, :edge]

            return carry

        lax.fori_loop(0, ref.shape[0] * RUNS, step, 0)


def first_kernel(layout, length, meta, *refs):
    *lefts, same_core, other_core, totals = refs
    totals[...] = jnp.zeros_like(totals)
    add_panels(layout, length, meta, lefts, same_core, other_core, totals)


def last_kernel(layout, length, meta, *refs):
    (*lefts, same_core, other_core, partial, base, next_hbm, sum_hbm,
     totals, next_buf, sum_buf, next_sem, sum_sem) = refs
    slots = totals.shape[0]
    totals[...] = partial[...]
    add_panels(layout, length, meta, lefts, same_core, other_core, totals)

    def out_copies(slot):
        return (
            pltpu.make_async_copy(next_buf.at[slot], next_hbm.at[slot], next_sem.at[slot]),
            pltpu.make_async_copy(sum_buf.at[slot], sum_hbm.at[slot], sum_sem.at[slot]),
        )

    for slot in range(slots):
        term = totals[slot] * SCALING
        next_buf[slot] = term.astype(jnp.bfloat16)
        sum_buf[slot] = base[slot] + term
        for copy in out_copies(slot):
            copy.start()
    for slot in range(slots):
        for copy in out_copies(slot):
            copy.wait()


def per_device(left_term, right_factor, targets, propagator_in):
    columns, rows = lax.axis_size("col"), lax.axis_size("row")
    edge = left_term.shape[4]
    slots = propagator_in.shape[2]
    length = columns // RUNS
    mine = left_term.reshape(2 * edge, edge)
    swap = [(c, (c + length) % columns) for c in range(columns)]

    other = lax.ppermute(mine, "col", swap)
    block = (slots, 2, edge, edge)
    in_vmem = pl.BlockSpec(memory_space=pltpu.VMEM)
    in_smem = pl.BlockSpec(memory_space=pltpu.SMEM)
    in_any = pl.BlockSpec(memory_space=pl.ANY)

    copies = pl.pallas_call(
        spread_kernel,
        out_shape=jax.ShapeDtypeStruct((rows // CORES, edge, 2 * edge), right_factor.dtype),
        in_specs=[in_vmem],
        out_specs=in_any,
        scratch_shapes=[pltpu.SemaphoreType.DMA((rows // CORES,))],
        cost_estimate=pl.CostEstimate(flops=0, bytes_accessed=8_000_000, transcendentals=0),
    )(right_factor[0, 0])
    column, row = lax.axis_index("col"), lax.axis_index("row")
    place = jnp.stack([column % length, column // length, row % CORES]).astype(jnp.int32)
    meta = jnp.concatenate([targets[0, 0, :, 0], place])
    other, copies, meta = lax.optimization_barrier((other, copies, meta))
    same_groups = [list(range(core, rows, CORES)) for core in range(CORES)]
    same_core = lax.all_to_all(copies, "row", 0, 0, axis_index_groups=same_groups)
    members = length // STRIDE
    groups = [
        [run * length + member * STRIDE + start for member in range(members)]
        for run in range(RUNS)
        for start in range(STRIDE)
    ]
    both = lax.all_gather(jnp.stack([mine, other]), "col", axis_index_groups=groups)
    low, high = both[: members // 2], both[members // 2 :]
    before, after2 = moved(low, columns, 1), moved(high, columns, -1)
    before2, after = moved(high, columns, 1), moved(low, columns, -1)
    far, far2 = moved(before, columns, 1), moved(after2, columns, -1)
    across = [(r, r ^ 1) for r in range(rows)]
    tied, _ = lax.optimization_barrier((same_core, both))
    other_core = lax.ppermute(tied, "row", across)
    half = members // 2
    early = [(both, (0, 0)), (before, (-1, 0)), (after2, (1, half)), (after, (1, 0)), (before2, (-1, half))]
    late = [(far, (-2, 0)), (far2, (2, half))]

    def first(*refs):
        first_kernel([g[1] for g in early], length, *refs)

    def last(*refs):
        last_kernel([g[1] for g in late], length, *refs)

    partial = pl.pallas_call(
        first,
        out_shape=jax.ShapeDtypeStruct(block, jnp.float32),
        in_specs=[in_smem] + [in_vmem] * (len(early) + 2),
        out_specs=in_vmem,
        compiler_params=pltpu.CompilerParams(vmem_limit_bytes=20 * 1024 * 1024),
        cost_estimate=pl.CostEstimate(flops=200_000_000, bytes_accessed=4_000_000, transcendentals=0),
    )(meta, *[g[0] for g in early], same_core, other_core)
    next_term, total = pl.pallas_call(
        last,
        out_shape=(
            jax.ShapeDtypeStruct(block, jnp.bfloat16),
            jax.ShapeDtypeStruct(block, jnp.float32),
        ),
        in_specs=[in_smem] + [in_vmem] * (len(late) + 4),
        out_specs=(in_any, in_any),
        scratch_shapes=[
            pltpu.VMEM(block, jnp.float32),
            pltpu.VMEM(block, jnp.bfloat16),
            pltpu.VMEM(block, jnp.float32),
            pltpu.SemaphoreType.DMA((slots,)),
            pltpu.SemaphoreType.DMA((slots,)),
        ],
        compiler_params=pltpu.CompilerParams(vmem_limit_bytes=20 * 1024 * 1024),
        cost_estimate=pl.CostEstimate(flops=100_000_000, bytes_accessed=4_000_000, transcendentals=0),
    )(meta, *[g[0] for g in late], same_core, other_core, partial, propagator_in.reshape(block))
    shape = propagator_in.shape
    return next_term.reshape(shape), total.reshape(shape)


def solution(mesh):
    in_specs = (
        P("row", "col", None, None, None, None),
        P("row", "col", None, None),
        P("row", "col", None, None),
        P("row", "col", None, None, None, None),
    )
    out_specs = (P("row", "col", None, None, None, None), P("row", "col", None, None, None, None))
    return jax.shard_map(
        per_device, mesh=mesh, in_specs=in_specs, out_specs=out_specs, check_vma=False
    )
```

time: 102 us -> 92.7 us (0.909)
  the two profiles are of different devices: /device:TPU:62 before, /device:TPU:1 now
where the time goes in v2:
time: 92.7 us; the launch traced here: 92.2 us
  starting transfers between devices  47 us (51%)
  blocking collectives  32.4 us (35%)
  waiting for transfers between devices  5.73 us (6%)
  Pallas kernels  5.48 us (6%)
    all_gather x1, blocking collectives, per_device(): lax.all_gather(jnp.stack([mine, other]), 'col', axis_index_groups=groups)  32.4 us
    ppermute x6, starting transfers between devices, moved(): return lax.ppermute(value, 'col', pairs)  24.8 us
    ppermute x1, starting transfers between devices, per_device(): other = lax.ppermute(mine, 'col', swap)  8.28 us
    all_to_all x1, starting transfers between devices, per_device(): lax.all_to_all(copies, 'row', 0, 0, axis_index_groups=same_groups)  7.2 us
    ppermute x1, starting transfers between devices, per_device(): other_core = lax.ppermute(tied, 'row', across)  6.73 us
    ppermute x6, waiting for transfers between devices, moved(): return lax.ppermute(value, 'col', pairs)  5.72 us
    pallas_call x1, Pallas kernels, per_device(): pl.pallas_call(last, out_shape=(jax.ShapeDtypeStruct(block, jnp.bfloat16)...  2.06 us
    pallas_call x1, Pallas kernels, per_device(): pl.pallas_call(spread_kernel, out_shape=jax.ShapeDtypeStruct((rows // COR...  1.93 us
  transfers between devices with their start and end apart: 9, of which 2 were waited for; matrix products, arithmetic and copies ran while one was open for 0% of the time, Pallas kernels for 4%

profile of v2, /device:TPU:1, one launch (start us, length us, event | category | flops | bytes accessed | tf_op | source)
XLA Modules:
  0.0 92.2 jit_solution(3428929528441761794)
XLA Ops:
  0.6 8.3 %collective-permute-start = (bf16[256,128]{1,0:T(8,128)(2,1)}, bf16[256,128]{1,0:T(8,128)(2,1)S(1)}, u32[]{:S(2)}, u32[]{:S(2)}) collective-permute-start(bf16[256,128]{1,0:T(8,128)(2,1)} %bitcast.21), channel_id=1, source_target_pairs={{0,16},{1,17},{2,18},{3,19},{4,20},{5,21},{6,22},{7,23},{8,24},{9,... | collective-permute-start | bytes 196616 | tf_op jit(solution)/shard_map/ppermute | solution.py:98
  8.9 1.9 %shard_map.59 = bf16[16,128,256]{2,1,0:T(8,128)(2,1)} custom-call(bf16[128,256]{1,0:T(8,128)(2,1)} %bitcast.20), custom_call_target="tpu_custom_call" | custom-call | bytes 8000000 | tf_op jit(solution)/shard_map/pallas_call | solution.py:104
  10.9 0.0 copy-start.2
  10.9 0.6 copy-done.2
  11.6 0.1 pad_add_fusion.refs_0_
  11.6 0.0 copy-start.1
  11.6 0.0 collective-permute-done
  11.6 7.2 %all-to-all-start = ((bf16[16,128,256]{2,1,0:T(8,128)(2,1)}), bf16[16,128,256]{2,1,0:T(8,128)(2,1)S(1)}, u32[]{:S(2)}, u32[]{:S(2)}) async-start(bf16[16,128,256]{2,1,0:T(8,128)(2,1)} %shard_map.59), calls=%async_computation | async-start | bytes 2097152 | tf_op jit(solution)/shard_map/all_to_all | solution.py:117
  18.9 0.0 copy-done.1
  18.9 32.4 %all-gather = bf16[8,256,128]{2,1,0:T(8,128)(2,1)S(1)} all-gather(bf16[2,256,128]{2,1,0:T(8,128)(2,1)S(1)} %pad_maximum_fusion), channel_id=2, replica_groups={{0,4,8,12},{1,5,9,13},{2,6,10,14},{3,7,11,15},{16,20,24,28},{17,21,25,2..., dimensions={0}, use_global_device_ids=true | all-gather | bytes 655360 | tf_op jit(solution)/shard_map/all_gather | solution.py:124
  51.3 0.0 all-to-all-done.refs_6_.refs_3_
  51.3 6.7 %collective-permute-start.5 = (bf16[16,128,256]{2,1,0:T(8,128)(2,1)S(1)}, bf16[16,128,256]{2,1,0:T(8,128)(2,1)S(1)}, u32[]{:S(2)}, u32[]{:S(2)}) collective-permute-start(bf16[16,128,256]{2,1,0:T(8,128)(2,1)S(1)} %all-to-all-done.refs_6_.refs_3_), channel_id=1, source_target_pairs={{0,32},{32,0},{64,96},{96,64},{128,160},{160,128},{192,224},{224,1... | collective-permute-start | bytes 3145736 | tf_op jit(solution)/shard_map/ppermute | solution.py:131
  58.1 3.3 %collective-permute-start.1 = (bf16[2,2,256,128]{3,2,1,0:T(8,128)(2,1)S(1)}, bf16[2,2,256,128]{3,2,1,0:T(8,128)(2,1)S(1)}, u32[]{:S(2)}, u32[]{:S(2)}) collective-permute-start(bf16[2,2,256,128]{3,2,1,0:T(8,128)(2,1)S(1)} %bitcast.18), channel_id=1, source_target_pairs={{0,1},{1,2},{2,3},{3,4},{4,5},{5,6},{6,7},{7,8},{8,9},{9,10},{10,1... | collective-permute-start | bytes 786440 | tf_op jit(solution)/shard_map/ppermute | solution.py:23
  61.4 0.0 copy-start
  61.4 9.7 %collective-permute-start.3 = (bf16[2,2,256,128]{3,2,1,0:T(8,128)(2,1)S(1)}, bf16[2,2,256,128]{3,2,1,0:T(8,128)(2,1)S(1)}, u32[]{:S(2)}, u32[]{:S(2)}) collective-permute-start(bf16[2,2,256,128]{3,2,1,0:T(8,128)(2,1)S(1)} %bitcast.16), channel_id=1, source_target_pairs={{0,15},{1,0},{2,1},{3,2},{4,3},{5,4},{6,5},{7,6},{8,7},{9,8},{10,9... | collective-permute-start | bytes 786440 | tf_op jit(solution)/shard_map/ppermute | solution.py:23
  71.1 3.4 %collective-permute-start.6 = (bf16[2,2,256,128]{3,2,1,0:T(8,128)(2,1)S(1)}, bf16[2,2,256,128]{3,2,1,0:T(8,128)(2,1)S(1)}, u32[]{:S(2)}, u32[]{:S(2)}) collective-permute-start(bf16[2,2,256,128]{3,2,1,0:T(8,128)(2,1)S(1)} %bitcast.19), channel_id=1, source_target_pairs={{0,15},{1,0},{2,1},{3,2},{4,3},{5,4},{6,5},{7,6},{8,7},{9,8},{10,9... | collective-permute-start | bytes 786440 | tf_op jit(solution)/shard_map/ppermute | solution.py:23
  74.5 1.9 %collective-permute-start.7 = (bf16[2,2,256,128]{3,2,1,0:T(8,128)(2,1)S(1)}, bf16[2,2,256,128]{3,2,1,0:T(8,128)(2,1)S(1)}, u32[]{:S(2)}, u32[]{:S(2)}) collective-permute-start(bf16[2,2,256,128]{3,2,1,0:T(8,128)(2,1)S(1)} %bitcast.17), channel_id=1, source_target_pairs={{0,1},{1,2},{2,3},{3,4},{4,5},{5,6},{6,7},{7,8},{8,9},{9,10},{10,1... | collective-permute-start | bytes 786440 | tf_op jit(solution)/shard_map/ppermute | solution.py:23
  76.4 0.0 collective-permute-done.1.refs_2_
  76.4 1.9 %collective-permute-start.2 = (bf16[2,2,256,128]{3,2,1,0:T(8,128)(2,1)S(1)}, bf16[2,2,256,128]{3,2,1,0:T(8,128)(2,1)S(1)}, u32[]{:S(2)}, u32[]{:S(2)}) collective-permute-start(bf16[2,2,256,128]{3,2,1,0:T(8,128)(2,1)S(1)} %collective-permute-done.1.refs_2_), channel_id=1, source_target_pairs={{0,1},{1,2},{2,3},{3,4},{4,5},{5,6},{6,7},{7,8},{8,9},{9,10},{10,1... | collective-permute-start | bytes 786440 | tf_op jit(solution)/shard_map/ppermute | solution.py:23
  78.4 0.0 collective-permute-done.3.refs_3_
  78.4 4.6 %collective-permute-start.4 = (bf16[2,2,256,128]{3,2,1,0:T(8,128)(2,1)S(1)}, bf16[2,2,256,128]{3,2,1,0:T(8,128)(2,1)S(1)}, u32[]{:S(2)}, u32[]{:S(2)}) collective-permute-start(bf16[2,2,256,128]{3,2,1,0:T(8,128)(2,1)S(1)} %collective-permute-done.3.refs_3_), channel_id=1, source_target_pairs={{0,15},{1,0},{2,1},{3,2},{4,3},{5,4},{6,5},{7,6},{8,7},{9,8},{10,9... | collective-permute-start | bytes 786440 | tf_op jit(solution)/shard_map/ppermute | solution.py:23
  82.9 0.0 collective-permute-done.6.refs_4_
  83.0 1.6 %collective-permute-done.7.refs_5_ = bf16[2,2,256,128]{3,2,1,0:T(8,128)(2,1)S(1)} collective-permute-done((bf16[2,2,256,128]{3,2,1,0:T(8,128)(2,1)S(1)}, bf16[2,2,256,128]{3,2,1,0:T(8,128)(2,1)S(1)}, u32[]{:S(2)}, u32[]{:S(2)}) %collective-permute-start.7) | collective-permute-done | bytes 262176 | tf_op jit(solution)/shard_map/ppermute | solution.py:23
  84.6 0.0 collective-permute-done.5.refs_7_.refs_4_
  84.6 1.5 %shard_map.60.refs_5_ = f32[8,2,128,128]{3,2,1,0:T(8,128)S(1)} custom-call(s32[35]{0:T(128)S(1)} %pad_add_fusion.refs_0_, bf16[4,2,256,128]{3,2,1,0:T(8,128)(2,1)S(1)} %bitcast.14, bf16[2,2,256,128]{3,2,1,0:T(8,128)(2,1)S(1)} %collective-permute-done.1.refs_2_, bf16[2,2,256,128]{3,2,1,0:T(8,128)(2,1)S(1)} %collective-permute-done.3.refs_3_, ...), custom_call_target="tpu_custom_call" | custom-call | flops 200000000 | bytes 4000000 | tf_op jit(solution)/shard_map/pallas_call | solution.py:142
  86.1 4.1 %collective-permute-done.2.refs_1_ = bf16[2,2,256,128]{3,2,1,0:T(8,128)(2,1)S(1)} collective-permute-done((bf16[2,2,256,128]{3,2,1,0:T(8,128)(2,1)S(1)}, bf16[2,2,256,128]{3,2,1,0:T(8,128)(2,1)S(1)}, u32[]{:S(2)}, u32[]{:S(2)}) %collective-permute-start.2) | collective-permute-done | bytes 262176 | tf_op jit(solution)/shard_map/ppermute | solution.py:23
  90.2 0.0 collective-permute-done.4.refs_2_
  90.2 0.0 copy-done
  90.2 2.1 %shard_map.61 = (bf16[8,2,128,128]{3,2,1,0:T(8,128)(2,1)}, f32[8,2,128,128]{3,2,1,0:T(8,128)}) custom-call(s32[35]{0:T(128)S(1)} %pad_add_fusion.refs_0_, bf16[2,2,256,128]{3,2,1,0:T(8,128)(2,1)S(1)} %collective-permute-done.2.refs_1_, bf16[2,2,256,128]{3,2,1,0:T(8,128)(2,1)S(1)} %collective-permute-done.4.refs_2_, ...), custom_call_target="tpu_custom_call" | custom-call | flops 100000000 | bytes 4000000 | tf_op jit(solution)/shard_map/pallas_call | solution.py:150
  (2 shorter events, 0.1 us)
Async XLA Ops:
  0.6 11.0 %collective-permute-start = (bf16[256,128]{1,0:T(8,128)(2,1)}, bf16[256,128]{1,0:T(8,128)(2,1)S(1)}, u32[]{:S(2)}, u32[]{:S(2)}) collective-permute-start(bf16[256,128]{1,0:T(8,128)(2,1)} %bitcast.21), channel_id=1, source_target_pairs={{0,16},{1,17},{2,18},{3,19},{4,20},{5,21},{6,22},{7,23},{8,24},{9,... | collective-permute-start | bytes 196616 | tf_op jit(solution)/shard_map/ppermute | solution.py:98
  10.9 0.7 copy-start.2
  11.6 7.2 %copy-start.1 = (bf16[1,1,1,2,128,128]{5,4,3,2,1,0:T(8,128)(2,1)S(1)}, bf16[1,1,1,2,128,128]{5,4,3,2,1,0:T(8,128)(2,1)}, u32[]{:S(2)}) copy-start(bf16[1,1,1,2,128,128]{5,4,3,2,1,0:T(8,128)(2,1)} %param.4) | copy-start | bytes 196612
  11.6 39.6 %all-to-all-start = ((bf16[16,128,256]{2,1,0:T(8,128)(2,1)}), bf16[16,128,256]{2,1,0:T(8,128)(2,1)S(1)}, u32[]{:S(2)}, u32[]{:S(2)}) async-start(bf16[16,128,256]{2,1,0:T(8,128)(2,1)} %shard_map.59), calls=%async_computation | async-start | bytes 2097152 | tf_op jit(solution)/shard_map/all_to_all | solution.py:117
  51.3 33.3 %collective-permute-start.5 = (bf16[16,128,256]{2,1,0:T(8,128)(2,1)S(1)}, bf16[16,128,256]{2,1,0:T(8,128)(2,1)S(1)}, u32[]{:S(2)}, u32[]{:S(2)}) collective-permute-start(bf16[16,128,256]{2,1,0:T(8,128)(2,1)S(1)} %all-to-all-done.refs_6_.refs_3_), channel_id=1, source_target_pairs={{0,32},{32,0},{64,96},{96,64},{128,160},{160,128},{192,224},{224,1... | collective-permute-start | bytes 3145736 | tf_op jit(solution)/shard_map/ppermute | solution.py:131
  58.1 18.4 %collective-permute-start.1 = (bf16[2,2,256,128]{3,2,1,0:T(8,128)(2,1)S(1)}, bf16[2,2,256,128]{3,2,1,0:T(8,128)(2,1)S(1)}, u32[]{:S(2)}, u32[]{:S(2)}) collective-permute-start(bf16[2,2,256,128]{3,2,1,0:T(8,128)(2,1)S(1)} %bitcast.18), channel_id=1, source_target_pairs={{0,1},{1,2},{2,3},{3,4},{4,5},{5,6},{6,7},{7,8},{8,9},{9,10},{10,1... | collective-permute-start | bytes 786440 | tf_op jit(solution)/shard_map/ppermute | solution.py:23
  61.4 28.8 %copy-start = (f32[1,1,8,2,128,128]{5,4,3,2,1,0:T(8,128)S(1)}, f32[1,1,8,2,128,128]{5,4,3,2,1,0:T(8,128)}, u32[]{:S(2)}) copy-start(f32[1,1,8,2,128,128]{5,4,3,2,1,0:T(8,128)} %param.7) | copy-start | bytes 3145732
  61.4 17.0 %collective-permute-start.3 = (bf16[2,2,256,128]{3,2,1,0:T(8,128)(2,1)S(1)}, bf16[2,2,256,128]{3,2,1,0:T(8,128)(2,1)S(1)}, u32[]{:S(2)}, u32[]{:S(2)}) collective-permute-start(bf16[2,2,256,128]{3,2,1,0:T(8,128)(2,1)S(1)} %bitcast.16), channel_id=1, source_target_pairs={{0,15},{1,0},{2,1},{3,2},{4,3},{5,4},{6,5},{7,6},{8,7},{9,8},{10,9... | collective-permute-start | bytes 786440 | tf_op jit(solution)/shard_map/ppermute | solution.py:23
  71.1 11.8 %collective-permute-start.6 = (bf16[2,2,256,128]{3,2,1,0:T(8,128)(2,1)S(1)}, bf16[2,2,256,128]{3,2,1,0:T(8,128)(2,1)S(1)}, u32[]{:S(2)}, u32[]{:S(2)}) collective-permute-start(bf16[2,2,256,128]{3,2,1,0:T(8,128)(2,1)S(1)} %bitcast.19), channel_id=1, source_target_pairs={{0,15},{1,0},{2,1},{3,2},{4,3},{5,4},{6,5},{7,6},{8,7},{9,8},{10,9... | collective-permute-start | bytes 786440 | tf_op jit(solution)/shard_map/ppermute | solution.py:23
  74.5 10.1 %collective-permute-start.7 = (bf16[2,2,256,128]{3,2,1,0:T(8,128)(2,1)S(1)}, bf16[2,2,256,128]{3,2,1,0:T(8,128)(2,1)S(1)}, u32[]{:S(2)}, u32[]{:S(2)}) collective-permute-start(bf16[2,2,256,128]{3,2,1,0:T(8,128)(2,1)S(1)} %bitcast.17), channel_id=1, source_target_pairs={{0,1},{1,2},{2,3},{3,4},{4,5},{5,6},{6,7},{7,8},{8,9},{9,10},{10,1... | collective-permute-start | bytes 786440 | tf_op jit(solution)/shard_map/ppermute | solution.py:23
  76.4 13.7 %collective-permute-start.2 = (bf16[2,2,256,128]{3,2,1,0:T(8,128)(2,1)S(1)}, bf16[2,2,256,128]{3,2,1,0:T(8,128)(2,1)S(1)}, u32[]{:S(2)}, u32[]{:S(2)}) collective-permute-start(bf16[2,2,256,128]{3,2,1,0:T(8,128)(2,1)S(1)} %collective-permute-done.1.refs_2_), channel_id=1, source_target_pairs={{0,1},{1,2},{2,3},{3,4},{4,5},{5,6},{6,7},{7,8},{8,9},{9,10},{10,1... | collective-permute-start | bytes 786440 | tf_op jit(solution)/shard_map/ppermute | solution.py:23
  78.4 11.8 %collective-permute-start.4 = (bf16[2,2,256,128]{3,2,1,0:T(8,128)(2,1)S(1)}, bf16[2,2,256,128]{3,2,1,0:T(8,128)(2,1)S(1)}, u32[]{:S(2)}, u32[]{:S(2)}) collective-permute-start(bf16[2,2,256,128]{3,2,1,0:T(8,128)(2,1)S(1)} %collective-permute-done.3.refs_3_), channel_id=1, source_target_pairs={{0,15},{1,0},{2,1},{3,2},{4,3},{5,4},{6,5},{7,6},{8,7},{9,8},{10,9... | collective-permute-start | bytes 786440 | tf_op jit(solution)/shard_map/ppermute | solution.py:23

commit v3 on v2

--- a/solution.py
+++ b/solution.py
@@ -31,7 +31,7 @@
         move.wait()
 
 
-def add_panels(layout, length, meta, lefts, same_core, other_core, totals):
+def add_panels(layout, length, meta, lefts, same_core, other_core, totals, touched=None):
     slots, edge = totals.shape[0], totals.shape[2]
     panels = RUNS * length
     place, my_run, my_core = meta[panels], meta[panels + 1], meta[panels + 2]
@@ -51,40 +51,63 @@
                 product = jnp.dot(ref[member, flip], block, preferred_element_type=jnp.float32)
                 totals[slot, 0] += product[:edge, edge:] + product[edge:, :edge]
                 totals[slot, 1] += product[edge:, edge:] - product[:edge, :edge]
+                if touched is not None:
+                    touched[slot] = 1
 
             return carry
 
         lax.fori_loop(0, ref.shape[0] * RUNS, step, 0)
 
 
+def out_copies(slot, next_buf, sum_buf, next_hbm, sum_hbm, next_sem, sum_sem):
+    return (
+        pltpu.make_async_copy(next_buf.at[slot], next_hbm.at[slot], next_sem.at[slot]),
+        pltpu.make_async_copy(sum_buf.at[slot], sum_hbm.at[slot], sum_sem.at[slot]),
+    )
+
+
+def write_slot(slot, totals, base, next_buf, sum_buf):
+    term = totals[slot] * SCALING
+    next_buf[slot] = term.astype(jnp.bfloat16)
+    sum_buf[slot] = base[slot] + term
+
+
 def first_kernel(layout, length, meta, *refs):
-    *lefts, same_core, other_core, totals = refs
+    (*lefts, same_core, other_core, base, totals, next_hbm, sum_hbm,
+     next_buf, sum_buf, next_sem, sum_sem) = refs
+    slots = totals.shape[0]
     totals[...] = jnp.zeros_like(totals)
     add_panels(layout, length, meta, lefts, same_core, other_core, totals)
+    for slot in range(slots):
+        write_slot(slot, totals, base, next_buf, sum_buf)
+        for copy in out_copies(slot, next_buf, sum_buf, next_hbm, sum_hbm, next_sem, sum_sem):
+            copy.start()
+    for slot in range(slots):
+        for copy in out_copies(slot, next_buf, sum_buf, next_hbm, sum_hbm, next_sem, sum_sem):
+            copy.wait()
 
 
 def last_kernel(layout, length, meta, *refs):
-    (*lefts, same_core, other_core, partial, base, next_hbm, sum_hbm,
-     totals, next_buf, sum_buf, next_sem, sum_sem) = refs
+    (*lefts, same_core, other_core, base, _, _, _, totals, next_hbm, sum_hbm,
+     touched, next_buf, sum_buf, next_sem, sum_sem) = refs
     slots = totals.shape[0]
-    totals[...] = partial[...]
-    add_panels(layout, length, meta, lefts, same_core, other_core, totals)
-
-    def out_copies(slot):
-        return (
-            pltpu.make_async_copy(next_buf.at[slot], next_hbm.at[slot], next_sem.at[slot]),
-            pltpu.make_async_copy(sum_buf.at[slot], sum_hbm.at[slot], sum_sem.at[slot]),
-        )
-
-    for slot in range(slots):
-        term = totals[slot] * SCALING
-        next_buf[slot] = term.astype(jnp.bfloat16)
-        sum_buf[slot] = base[slot] + term
-        for copy in out_copies(slot):
-            copy.start()
-    for slot in range(slots):
-        for copy in out_copies(slot):
-            copy.wait()
+    for slot in range(slots):
+        touched[slot] = 0
+    add_panels(layout, length, meta, lefts, same_core, other_core, totals, touched)
+    for slot in range(slots):
+
+        @pl.when(touched[slot] == 1)
+        def _():
+            write_slot(slot, totals, base, next_buf, sum_buf)
+            for copy in out_copies(slot, next_buf, sum_buf, next_hbm, sum_hbm, next_sem, sum_sem):
+                copy.start()
+
+    for slot in range(slots):
+
+        @pl.when(touched[slot] == 1)
+        def _():
+            for copy in out_copies(slot, next_buf, sum_buf, next_hbm, sum_hbm, next_sem, sum_sem):
+                copy.wait()
 
 
 def per_device(left_term, right_factor, targets, propagator_in):
@@ -107,7 +130,7 @@
         in_specs=[in_vmem],
         out_specs=in_any,
         scratch_shapes=[pltpu.SemaphoreType.DMA((rows // CORES,))],
-        cost_estimate=pl.CostEstimate(flops=0, bytes_accessed=8_000_000, transcendentals=0),
+        cost_estimate=pl.CostEstimate(flops=0, bytes_accessed=1_114_112, transcendentals=0),
     )(right_factor[0, 0])
     column, row = lax.axis_index("col"), lax.axis_index("row")
     place = jnp.stack([column % length, column // length, row % CORES]).astype(jnp.int32)
@@ -139,32 +162,37 @@
     def last(*refs):
         last_kernel([g[1] for g in late], length, *refs)
 
-    partial = pl.pallas_call(
+    base = propagator_in.reshape(block)
+    out_shape = (
+        jax.ShapeDtypeStruct(block, jnp.float32),
+        jax.ShapeDtypeStruct(block, jnp.bfloat16),
+        jax.ShapeDtypeStruct(block, jnp.float32),
+    )
+    buffers = [
+        pltpu.VMEM(block, jnp.bfloat16),
+        pltpu.VMEM(block, jnp.float32),
+        pltpu.SemaphoreType.DMA((slots,)),
+        pltpu.SemaphoreType.DMA((slots,)),
+    ]
+    partial, next_term, total = pl.pallas_call(
         first,
-        out_shape=jax.ShapeDtypeStruct(block, jnp.float32),
-        in_specs=[in_smem] + [in_vmem] * (len(early) + 2),
-        out_specs=in_vmem,
+        out_shape=out_shape,
+        in_specs=[in_smem] + [in_vmem] * (len(early) + 3),
+        out_specs=(in_vmem, in_any, in_any),
+        scratch_shapes=buffers,
         compiler_params=pltpu.CompilerParams(vmem_limit_bytes=20 * 1024 * 1024),
         cost_estimate=pl.CostEstimate(flops=200_000_000, bytes_accessed=4_000_000, transcendentals=0),
-    )(meta, *[g[0] for g in early], same_core, other_core)
-    next_term, total = pl.pallas_call(
+    )(meta, *[g[0] for g in early], same_core, other_core, base)
+    _, next_term, total = pl.pallas_call(
         last,
-        out_shape=(
-            jax.ShapeDtypeStruct(block, jnp.bfloat16),
-            jax.ShapeDtypeStruct(block, jnp.float32),
-        ),
-        in_specs=[in_smem] + [in_vmem] * (len(late) + 4),
-        out_specs=(in_any, in_any),
-        scratch_shapes=[
-            pltpu.VMEM(block, jnp.float32),
-            pltpu.VMEM(block, jnp.bfloat16),
-            pltpu.VMEM(block, jnp.float32),
-            pltpu.SemaphoreType.DMA((slots,)),
-            pltpu.SemaphoreType.DMA((slots,)),
-        ],
+        out_shape=out_shape,
+        in_specs=[in_smem] + [in_vmem] * (len(late) + 4) + [in_any, in_any],
+        out_specs=(in_vmem, in_any, in_any),
+        scratch_shapes=[pltpu.SMEM((slots,), jnp.int32)] + buffers,
+        input_output_aliases={len(late) + 4 + i: i for i in range(3)},
         compiler_params=pltpu.CompilerParams(vmem_limit_bytes=20 * 1024 * 1024),
-        cost_estimate=pl.CostEstimate(flops=100_000_000, bytes_accessed=4_000_000, transcendentals=0),
-    )(meta, *[g[0] for g in late], same_core, other_core, partial, propagator_in.reshape(block))
+        cost_estimate=pl.CostEstimate(flops=70_000_000, bytes_accessed=2_000_000, transcendentals=0),
+    )(meta, *[g[0] for g in late], same_core, other_core, base, partial, next_term, total)
     shape = propagator_in.shape
     return next_term.reshape(shape), total.reshape(shape)
 

time: 92.7 us -> 92.3 us (level)
  waiting for transfers between devices: 5.73 us -> 4.63 us
    ppermute x6, waiting for transfers between devices: 5.72 us -> 4.62 us  [moved(): return lax.ppermute(value, 'col', pairs)]
  transfers between devices with their start and end apart: 9 -> 9, of which waited for: 2 -> 2; matrix products, arithmetic and copies ran while one was open for 0% -> 0% of each run, Pallas kernels for 4% -> 5%
where the time goes in v3:
time: 92.3 us; the launch traced here: 92 us
  starting transfers between devices  46.9 us (51%)
  blocking collectives  32.5 us (35%)
  Pallas kernels  6.31 us (7%)
  waiting for transfers between devices  4.63 us (5%)
    all_gather x1, blocking collectives, per_device(): lax.all_gather(jnp.stack([mine, other]), 'col', axis_index_groups=groups)  32.5 us
    ppermute x6, starting transfers between devices, moved(): return lax.ppermute(value, 'col', pairs)  24.7 us
    ppermute x1, starting transfers between devices, per_device(): other = lax.ppermute(mine, 'col', swap)  8.28 us
    all_to_all x1, starting transfers between devices, per_device(): lax.all_to_all(copies, 'row', 0, 0, axis_index_groups=same_groups)  7.2 us
    ppermute x1, starting transfers between devices, per_device(): other_core = lax.ppermute(tied, 'row', across)  6.73 us
    ppermute x6, waiting for transfers between devices, moved(): return lax.ppermute(value, 'col', pairs)  4.62 us
    pallas_call x1, Pallas kernels, per_device(): pl.pallas_call(first, out_shape=out_shape, in_specs=[in_smem] + [in_vmem]...  2.59 us
    pallas_call x1, Pallas kernels, per_device(): pl.pallas_call(spread_kernel, out_shape=jax.ShapeDtypeStruct((rows // COR...  1.93 us
  transfers between devices with their start and end apart: 9, of which 2 were waited for; matrix products, arithmetic and copies ran while one was open for 0% of the time, Pallas kernels for 5%

profile of v3, /device:TPU:1, one launch (start us, length us, event | category | flops | bytes accessed | tf_op | source)
XLA Modules:
  0.0 92.0 jit_solution(13450499092808553713)
XLA Ops:
  0.6 8.3 %collective-permute-start = (bf16[256,128]{1,0:T(8,128)(2,1)}, bf16[256,128]{1,0:T(8,128)(2,1)S(1)}, u32[]{:S(2)}, u32[]{:S(2)}) collective-permute-start(bf16[256,128]{1,0:T(8,128)(2,1)} %bitcast.24), channel_id=1, source_target_pairs={{0,16},{1,17},{2,18},{3,19},{4,20},{5,21},{6,22},{7,23},{8,24},{9,... | collective-permute-start | bytes 196616 | tf_op jit(solution)/shard_map/ppermute | solution.py:121
  8.9 1.9 %shard_map.59 = bf16[16,128,256]{2,1,0:T(8,128)(2,1)} custom-call(bf16[128,256]{1,0:T(8,128)(2,1)} %bitcast.23), custom_call_target="tpu_custom_call" | custom-call | bytes 1114112 | tf_op jit(solution)/shard_map/pallas_call | solution.py:127
  10.9 0.0 copy-start.2
  10.9 0.6 copy-done.2
  11.6 0.1 pad_add_fusion.refs_0_
  11.6 0.0 copy-start.1
  11.6 0.0 collective-permute-done
  11.6 7.2 %all-to-all-start = ((bf16[16,128,256]{2,1,0:T(8,128)(2,1)}), bf16[16,128,256]{2,1,0:T(8,128)(2,1)S(1)}, u32[]{:S(2)}, u32[]{:S(2)}) async-start(bf16[16,128,256]{2,1,0:T(8,128)(2,1)} %shard_map.59), calls=%async_computation | async-start | bytes 2097152 | tf_op jit(solution)/shard_map/all_to_all | solution.py:140
  18.9 0.0 copy-start
  18.9 0.0 copy-done.1
  18.9 32.5 %all-gather = bf16[8,256,128]{2,1,0:T(8,128)(2,1)S(1)} all-gather(bf16[2,256,128]{2,1,0:T(8,128)(2,1)S(1)} %pad_maximum_fusion), channel_id=2, replica_groups={{0,4,8,12},{1,5,9,13},{2,6,10,14},{3,7,11,15},{16,20,24,28},{17,21,25,2..., dimensions={0}, use_global_device_ids=true | all-gather | bytes 655360 | tf_op jit(solution)/shard_map/all_gather | solution.py:147
  51.4 0.0 all-to-all-done.refs_6_.refs_3_
  51.4 6.7 %collective-permute-start.5 = (bf16[16,128,256]{2,1,0:T(8,128)(2,1)S(1)}, bf16[16,128,256]{2,1,0:T(8,128)(2,1)S(1)}, u32[]{:S(2)}, u32[]{:S(2)}) collective-permute-start(bf16[16,128,256]{2,1,0:T(8,128)(2,1)S(1)} %all-to-all-done.refs_6_.refs_3_), channel_id=1, source_target_pairs={{0,32},{32,0},{64,96},{96,64},{128,160},{160,128},{192,224},{224,1... | collective-permute-start | bytes 3145736 | tf_op jit(solution)/shard_map/ppermute | solution.py:154
  58.2 3.3 %collective-permute-start.1 = (bf16[2,2,256,128]{3,2,1,0:T(8,128)(2,1)S(1)}, bf16[2,2,256,128]{3,2,1,0:T(8,128)(2,1)S(1)}, u32[]{:S(2)}, u32[]{:S(2)}) collective-permute-start(bf16[2,2,256,128]{3,2,1,0:T(8,128)(2,1)S(1)} %bitcast.21), channel_id=1, source_target_pairs={{0,1},{1,2},{2,3},{3,4},{4,5},{5,6},{6,7},{7,8},{8,9},{9,10},{10,1... | collective-permute-start | bytes 786440 | tf_op jit(solution)/shard_map/ppermute | solution.py:23
  61.5 9.6 %collective-permute-start.3 = (bf16[2,2,256,128]{3,2,1,0:T(8,128)(2,1)S(1)}, bf16[2,2,256,128]{3,2,1,0:T(8,128)(2,1)S(1)}, u32[]{:S(2)}, u32[]{:S(2)}) collective-permute-start(bf16[2,2,256,128]{3,2,1,0:T(8,128)(2,1)S(1)} %bitcast.19), channel_id=1, source_target_pairs={{0,15},{1,0},{2,1},{3,2},{4,3},{5,4},{6,5},{7,6},{8,7},{9,8},{10,9... | collective-permute-start | bytes 786440 | tf_op jit(solution)/shard_map/ppermute | solution.py:23
  71.1 3.4 %collective-permute-start.6 = (bf16[2,2,256,128]{3,2,1,0:T(8,128)(2,1)S(1)}, bf16[2,2,256,128]{3,2,1,0:T(8,128)(2,1)S(1)}, u32[]{:S(2)}, u32[]{:S(2)}) collective-permute-start(bf16[2,2,256,128]{3,2,1,0:T(8,128)(2,1)S(1)} %bitcast.22), channel_id=1, source_target_pairs={{0,15},{1,0},{2,1},{3,2},{4,3},{5,4},{6,5},{7,6},{8,7},{9,8},{10,9... | collective-permute-start | bytes 786440 | tf_op jit(solution)/shard_map/ppermute | solution.py:23
  74.5 1.9 %collective-permute-start.7 = (bf16[2,2,256,128]{3,2,1,0:T(8,128)(2,1)S(1)}, bf16[2,2,256,128]{3,2,1,0:T(8,128)(2,1)S(1)}, u32[]{:S(2)}, u32[]{:S(2)}) collective-permute-start(bf16[2,2,256,128]{3,2,1,0:T(8,128)(2,1)S(1)} %bitcast.20), channel_id=1, source_target_pairs={{0,1},{1,2},{2,3},{3,4},{4,5},{5,6},{6,7},{7,8},{8,9},{9,10},{10,1... | collective-permute-start | bytes 786440 | tf_op jit(solution)/shard_map/ppermute | solution.py:23
  76.4 0.0 collective-permute-done.1.refs_2_
  76.4 1.9 %collective-permute-start.2 = (bf16[2,2,256,128]{3,2,1,0:T(8,128)(2,1)S(1)}, bf16[2,2,256,128]{3,2,1,0:T(8,128)(2,1)S(1)}, u32[]{:S(2)}, u32[]{:S(2)}) collective-permute-start(bf16[2,2,256,128]{3,2,1,0:T(8,128)(2,1)S(1)} %collective-permute-done.1.refs_2_), channel_id=1, source_target_pairs={{0,1},{1,2},{2,3},{3,4},{4,5},{5,6},{6,7},{7,8},{8,9},{9,10},{10,1... | collective-permute-start | bytes 786440 | tf_op jit(solution)/shard_map/ppermute | solution.py:23
  78.4 0.0 collective-permute-done.3.refs_3_
  78.4 4.6 %collective-permute-start.4 = (bf16[2,2,256,128]{3,2,1,0:T(8,128)(2,1)S(1)}, bf16[2,2,256,128]{3,2,1,0:T(8,128)(2,1)S(1)}, u32[]{:S(2)}, u32[]{:S(2)}) collective-permute-start(bf16[2,2,256,128]{3,2,1,0:T(8,128)(2,1)S(1)} %collective-permute-done.3.refs_3_), channel_id=1, source_target_pairs={{0,15},{1,0},{2,1},{3,2},{4,3},{5,4},{6,5},{7,6},{8,7},{9,8},{10,9... | collective-permute-start | bytes 786440 | tf_op jit(solution)/shard_map/ppermute | solution.py:23
  82.9 0.0 collective-permute-done.6.refs_4_
  83.0 1.6 %collective-permute-done.7.refs_5_ = bf16[2,2,256,128]{3,2,1,0:T(8,128)(2,1)S(1)} collective-permute-done((bf16[2,2,256,128]{3,2,1,0:T(8,128)(2,1)S(1)}, bf16[2,2,256,128]{3,2,1,0:T(8,128)(2,1)S(1)}, u32[]{:S(2)}, u32[]{:S(2)}) %collective-permute-start.7) | collective-permute-done | bytes 262176 | tf_op jit(solution)/shard_map/ppermute | solution.py:23
  84.6 0.0 collective-permute-done.5.refs_7_.refs_4_
  84.6 0.0 copy-done
  84.6 2.6 %shard_map.60 = (f32[8,2,128,128]{3,2,1,0:T(8,128)S(1)}, bf16[8,2,128,128]{3,2,1,0:T(8,128)(2,1)}, f32[8,2,128,128]{3,2,1,0:T(8,128)}) custom-call(s32[35]{0:T(128)S(1)} %pad_add_fusion.refs_0_, bf16[4,2,256,128]{3,2,1,0:T(8,128)(2,1)S(1)} %bitcast.14, bf16[2,2,256,128]{3,2,1,0:T(8,128)(2,1)S(1)} %collective-permute-done.1.refs_2_, ...), custom_call_target="tpu_custom_call" | custom-call | flops 200000000 | bytes 4000000 | tf_op jit(solution)/shard_map/pallas_call | solution.py:177
  87.2 3.0 %collective-permute-done.2.refs_1_ = bf16[2,2,256,128]{3,2,1,0:T(8,128)(2,1)S(1)} collective-permute-done((bf16[2,2,256,128]{3,2,1,0:T(8,128)(2,1)S(1)}, bf16[2,2,256,128]{3,2,1,0:T(8,128)(2,1)S(1)}, u32[]{:S(2)}, u32[]{:S(2)}) %collective-permute-start.2) | collective-permute-done | bytes 262176 | tf_op jit(solution)/shard_map/ppermute | solution.py:23
  90.2 0.0 collective-permute-done.4.refs_2_
  90.2 1.8 %shard_map.61 = (f32[8,2,128,128]{3,2,1,0:T(8,128)S(1)}, bf16[8,2,128,128]{3,2,1,0:T(8,128)(2,1)}, f32[8,2,128,128]{3,2,1,0:T(8,128)}) custom-call(s32[35]{0:T(128)S(1)} %pad_add_fusion.refs_0_, bf16[2,2,256,128]{3,2,1,0:T(8,128)(2,1)S(1)} %collective-permute-done.2.refs_1_, ...), custom_call_target="tpu_custom_call", output_to_operand_aliasing={{0}: (6, {}), {1}: (7, {}), {2}: (8, {})} | custom-call | flops 70000000 | bytes 2000000 | tf_op jit(solution)/shard_map/pallas_call | solution.py:186
  (2 shorter events, 0.1 us)
Async XLA Ops:
  0.6 11.0 %collective-permute-start = (bf16[256,128]{1,0:T(8,128)(2,1)}, bf16[256,128]{1,0:T(8,128)(2,1)S(1)}, u32[]{:S(2)}, u32[]{:S(2)}) collective-permute-start(bf16[256,128]{1,0:T(8,128)(2,1)} %bitcast.24), channel_id=1, source_target_pairs={{0,16},{1,17},{2,18},{3,19},{4,20},{5,21},{6,22},{7,23},{8,24},{9,... | collective-permute-start | bytes 196616 | tf_op jit(solution)/shard_map/ppermute | solution.py:121
  10.9 0.7 copy-start.2
  11.6 7.2 %copy-start.1 = (bf16[1,1,1,2,128,128]{5,4,3,2,1,0:T(8,128)(2,1)S(1)}, bf16[1,1,1,2,128,128]{5,4,3,2,1,0:T(8,128)(2,1)}, u32[]{:S(2)}) copy-start(bf16[1,1,1,2,128,128]{5,4,3,2,1,0:T(8,128)(2,1)} %param.4) | copy-start | bytes 196612
  11.6 39.8 %all-to-all-start = ((bf16[16,128,256]{2,1,0:T(8,128)(2,1)}), bf16[16,128,256]{2,1,0:T(8,128)(2,1)S(1)}, u32[]{:S(2)}, u32[]{:S(2)}) async-start(bf16[16,128,256]{2,1,0:T(8,128)(2,1)} %shard_map.59), calls=%async_computation | async-start | bytes 2097152 | tf_op jit(solution)/shard_map/all_to_all | solution.py:140
  18.9 65.7 %copy-start = (f32[1,1,8,2,128,128]{5,4,3,2,1,0:T(8,128)S(1)}, f32[1,1,8,2,128,128]{5,4,3,2,1,0:T(8,128)}, u32[]{:S(2)}) copy-start(f32[1,1,8,2,128,128]{5,4,3,2,1,0:T(8,128)} %param.7) | copy-start | bytes 3145732
  51.4 33.1 %collective-permute-start.5 = (bf16[16,128,256]{2,1,0:T(8,128)(2,1)S(1)}, bf16[16,128,256]{2,1,0:T(8,128)(2,1)S(1)}, u32[]{:S(2)}, u32[]{:S(2)}) collective-permute-start(bf16[16,128,256]{2,1,0:T(8,128)(2,1)S(1)} %all-to-all-done.refs_6_.refs_3_), channel_id=1, source_target_pairs={{0,32},{32,0},{64,96},{96,64},{128,160},{160,128},{192,224},{224,1... | collective-permute-start | bytes 3145736 | tf_op jit(solution)/shard_map/ppermute | solution.py:154
  58.2 18.2 %collective-permute-start.1 = (bf16[2,2,256,128]{3,2,1,0:T(8,128)(2,1)S(1)}, bf16[2,2,256,128]{3,2,1,0:T(8,128)(2,1)S(1)}, u32[]{:S(2)}, u32[]{:S(2)}) collective-permute-start(bf16[2,2,256,128]{3,2,1,0:T(8,128)(2,1)S(1)} %bitcast.21), channel_id=1, source_target_pairs={{0,1},{1,2},{2,3},{3,4},{4,5},{5,6},{6,7},{7,8},{8,9},{9,10},{10,1... | collective-permute-start | bytes 786440 | tf_op jit(solution)/shard_map/ppermute | solution.py:23
  61.5 16.8 %collective-permute-start.3 = (bf16[2,2,256,128]{3,2,1,0:T(8,128)(2,1)S(1)}, bf16[2,2,256,128]{3,2,1,0:T(8,128)(2,1)S(1)}, u32[]{:S(2)}, u32[]{:S(2)}) collective-permute-start(bf16[2,2,256,128]{3,2,1,0:T(8,128)(2,1)S(1)} %bitcast.19), channel_id=1, source_target_pairs={{0,15},{1,0},{2,1},{3,2},{4,3},{5,4},{6,5},{7,6},{8,7},{9,8},{10,9... | collective-permute-start | bytes 786440 | tf_op jit(solution)/shard_map/ppermute | solution.py:23
  71.1 11.8 %collective-permute-start.6 = (bf16[2,2,256,128]{3,2,1,0:T(8,128)(2,1)S(1)}, bf16[2,2,256,128]{3,2,1,0:T(8,128)(2,1)S(1)}, u32[]{:S(2)}, u32[]{:S(2)}) collective-permute-start(bf16[2,2,256,128]{3,2,1,0:T(8,128)(2,1)S(1)} %bitcast.22), channel_id=1, source_target_pairs={{0,15},{1,0},{2,1},{3,2},{4,3},{5,4},{6,5},{7,6},{8,7},{9,8},{10,9... | collective-permute-start | bytes 786440 | tf_op jit(solution)/shard_map/ppermute | solution.py:23
  74.5 10.1 %collective-permute-start.7 = (bf16[2,2,256,128]{3,2,1,0:T(8,128)(2,1)S(1)}, bf16[2,2,256,128]{3,2,1,0:T(8,128)(2,1)S(1)}, u32[]{:S(2)}, u32[]{:S(2)}) collective-permute-start(bf16[2,2,256,128]{3,2,1,0:T(8,128)(2,1)S(1)} %bitcast.20), channel_id=1, source_target_pairs={{0,1},{1,2},{2,3},{3,4},{4,5},{5,6},{6,7},{7,8},{8,9},{9,10},{10,1... | collective-permute-start | bytes 786440 | tf_op jit(solution)/shard_map/ppermute | solution.py:23
  76.4 13.7 %collective-permute-start.2 = (bf16[2,2,256,128]{3,2,1,0:T(8,128)(2,1)S(1)}, bf16[2,2,256,128]{3,2,1,0:T(8,128)(2,1)S(1)}, u32[]{:S(2)}, u32[]{:S(2)}) collective-permute-start(bf16[2,2,256,128]{3,2,1,0:T(8,128)(2,1)S(1)} %collective-permute-done.1.refs_2_), channel_id=1, source_target_pairs={{0,1},{1,2},{2,3},{3,4},{4,5},{5,6},{6,7},{7,8},{8,9},{9,10},{10,1... | collective-permute-start | bytes 786440 | tf_op jit(solution)/shard_map/ppermute | solution.py:23
  78.4 11.8 %collective-permute-start.4 = (bf16[2,2,256,128]{3,2,1,0:T(8,128)(2,1)S(1)}, bf16[2,2,256,128]{3,2,1,0:T(8,128)(2,1)S(1)}, u32[]{:S(2)}, u32[]{:S(2)}) collective-permute-start(bf16[2,2,256,128]{3,2,1,0:T(8,128)(2,1)S(1)} %collective-permute-done.3.refs_3_), channel_id=1, source_target_pairs={{0,15},{1,0},{2,1},{3,2},{4,3},{5,4},{6,5},{7,6},{8,7},{9,8},{10,9... | collective-permute-start | bytes 786440 | tf_op jit(solution)/shard_map/ppermute | solution.py:23

commit v4 on v3

--- a/solution.py
+++ b/solution.py
@@ -128,7 +128,7 @@
         spread_kernel,
         out_shape=jax.ShapeDtypeStruct((rows // CORES, edge, 2 * edge), right_factor.dtype),
         in_specs=[in_vmem],
-        out_specs=in_any,
+        out_specs=in_vmem,
         scratch_shapes=[pltpu.SemaphoreType.DMA((rows // CORES,))],
         cost_estimate=pl.CostEstimate(flops=0, bytes_accessed=1_114_112, transcendentals=0),
     )(right_factor[0, 0])

time: 92.3 us -> 92.5 us (level)
  starting transfers between devices: 46.9 us -> 45.5 us
  Pallas kernels: 6.31 us -> 7.64 us
    pallas_call x1, Pallas kernels: 1.93 us -> 3.29 us  [per_device(): pl.pallas_call(spread_kernel, out_shape=jax.ShapeDtypeStruct((rows // COR...]
    all_to_all x1, starting transfers between devices: 7.2 us -> 5.84 us  [per_device(): lax.all_to_all(copies, 'row', 0, 0, axis_index_groups=same_groups)]
  transfers between devices with their start and end apart: 9 -> 9, of which waited for: 2 -> 2; matrix products, arithmetic and copies ran while one was open for 0% -> 0% of each run, Pallas kernels for 5% -> 6%
where the time goes in v4:
time: 92.5 us; the launch traced here: 91.9 us
  starting transfers between devices  45.5 us (49%)
  blocking collectives  32.5 us (35%)
  Pallas kernels  7.64 us (8%)
  waiting for transfers between devices  4.63 us (5%)
    all_gather x1, blocking collectives, per_device(): lax.all_gather(jnp.stack([mine, other]), 'col', axis_index_groups=groups)  32.5 us
    ppermute x6, starting transfers between devices, moved(): return lax.ppermute(value, 'col', pairs)  24.7 us
    ppermute x1, starting transfers between devices, per_device(): other = lax.ppermute(mine, 'col', swap)  8.28 us
    ppermute x1, starting transfers between devices, per_device(): other_core = lax.ppermute(tied, 'row', across)  6.73 us
    all_to_all x1, starting transfers between devices, per_device(): lax.all_to_all(copies, 'row', 0, 0, axis_index_groups=same_groups)  5.84 us
    ppermute x6, waiting for transfers between devices, moved(): return lax.ppermute(value, 'col', pairs)  4.62 us
    pallas_call x1, Pallas kernels, per_device(): pl.pallas_call(spread_kernel, out_shape=jax.ShapeDtypeStruct((rows // COR...  3.29 us
    pallas_call x1, Pallas kernels, per_device(): pl.pallas_call(first, out_shape=out_shape, in_specs=[in_smem] + [in_vmem]...  2.59 us
  transfers between devices with their start and end apart: 9, of which 2 were waited for; matrix products, arithmetic and copies ran while one was open for 0% of the time, Pallas kernels for 6%

profile of v4, /device:TPU:1, one launch (start us, length us, event | category | flops | bytes accessed | tf_op | source)
XLA Modules:
  0.0 91.9 jit_solution(16967812809207494731)
XLA Ops:
  0.6 8.3 %collective-permute-start = (bf16[256,128]{1,0:T(8,128)(2,1)}, bf16[256,128]{1,0:T(8,128)(2,1)S(1)}, u32[]{:S(2)}, u32[]{:S(2)}) collective-permute-start(bf16[256,128]{1,0:T(8,128)(2,1)} %bitcast.24), channel_id=1, source_target_pairs={{0,16},{1,17},{2,18},{3,19},{4,20},{5,21},{6,22},{7,23},{8,24},{9,... | collective-permute-start | bytes 196616 | tf_op jit(solution)/shard_map/ppermute | solution.py:121
  8.9 3.3 %shard_map.59 = bf16[16,128,256]{2,1,0:T(8,128)(2,1)} custom-call(bf16[128,256]{1,0:T(8,128)(2,1)} %bitcast.23), custom_call_target="tpu_custom_call" | custom-call | bytes 1114112 | tf_op jit(solution)/shard_map/pallas_call | solution.py:127
  12.3 0.0 copy-start.2
  12.3 0.6 copy-done.2
  12.9 0.1 pad_add_fusion.refs_0_
  13.0 0.0 copy-start.1
  13.0 0.0 collective-permute-done
  13.0 5.8 %all-to-all-start = ((bf16[16,128,256]{2,1,0:T(8,128)(2,1)}), bf16[16,128,256]{2,1,0:T(8,128)(2,1)S(1)}, u32[]{:S(2)}, u32[]{:S(2)}) async-start(bf16[16,128,256]{2,1,0:T(8,128)(2,1)} %shard_map.59), calls=%async_computation | async-start | bytes 2097152 | tf_op jit(solution)/shard_map/all_to_all | solution.py:140
  18.9 0.0 copy-start
  18.9 0.0 copy-done.1
  18.9 32.5 %all-gather = bf16[8,256,128]{2,1,0:T(8,128)(2,1)S(1)} all-gather(bf16[2,256,128]{2,1,0:T(8,128)(2,1)S(1)} %pad_maximum_fusion), channel_id=2, replica_groups={{0,4,8,12},{1,5,9,13},{2,6,10,14},{3,7,11,15},{16,20,24,28},{17,21,25,2..., dimensions={0}, use_global_device_ids=true | all-gather | bytes 655360 | tf_op jit(solution)/shard_map/all_gather | solution.py:147
  51.4 0.0 all-to-all-done.refs_6_.refs_3_
  51.4 6.7 %collective-permute-start.5 = (bf16[16,128,256]{2,1,0:T(8,128)(2,1)S(1)}, bf16[16,128,256]{2,1,0:T(8,128)(2,1)S(1)}, u32[]{:S(2)}, u32[]{:S(2)}) collective-permute-start(bf16[16,128,256]{2,1,0:T(8,128)(2,1)S(1)} %all-to-all-done.refs_6_.refs_3_), channel_id=1, source_target_pairs={{0,32},{32,0},{64,96},{96,64},{128,160},{160,128},{192,224},{224,1... | collective-permute-start | bytes 3145736 | tf_op jit(solution)/shard_map/ppermute | solution.py:154
  58.2 3.3 %collective-permute-start.1 = (bf16[2,2,256,128]{3,2,1,0:T(8,128)(2,1)S(1)}, bf16[2,2,256,128]{3,2,1,0:T(8,128)(2,1)S(1)}, u32[]{:S(2)}, u32[]{:S(2)}) collective-permute-start(bf16[2,2,256,128]{3,2,1,0:T(8,128)(2,1)S(1)} %bitcast.21), channel_id=1, source_target_pairs={{0,1},{1,2},{2,3},{3,4},{4,5},{5,6},{6,7},{7,8},{8,9},{9,10},{10,1... | collective-permute-start | bytes 786440 | tf_op jit(solution)/shard_map/ppermute | solution.py:23
  61.5 9.6 %collective-permute-start.3 = (bf16[2,2,256,128]{3,2,1,0:T(8,128)(2,1)S(1)}, bf16[2,2,256,128]{3,2,1,0:T(8,128)(2,1)S(1)}, u32[]{:S(2)}, u32[]{:S(2)}) collective-permute-start(bf16[2,2,256,128]{3,2,1,0:T(8,128)(2,1)S(1)} %bitcast.19), channel_id=1, source_target_pairs={{0,15},{1,0},{2,1},{3,2},{4,3},{5,4},{6,5},{7,6},{8,7},{9,8},{10,9... | collective-permute-start | bytes 786440 | tf_op jit(solution)/shard_map/ppermute | solution.py:23
  71.1 3.4 %collective-permute-start.6 = (bf16[2,2,256,128]{3,2,1,0:T(8,128)(2,1)S(1)}, bf16[2,2,256,128]{3,2,1,0:T(8,128)(2,1)S(1)}, u32[]{:S(2)}, u32[]{:S(2)}) collective-permute-start(bf16[2,2,256,128]{3,2,1,0:T(8,128)(2,1)S(1)} %bitcast.22), channel_id=1, source_target_pairs={{0,15},{1,0},{2,1},{3,2},{4,3},{5,4},{6,5},{7,6},{8,7},{9,8},{10,9... | collective-permute-start | bytes 786440 | tf_op jit(solution)/shard_map/ppermute | solution.py:23
  74.5 1.9 %collective-permute-start.7 = (bf16[2,2,256,128]{3,2,1,0:T(8,128)(2,1)S(1)}, bf16[2,2,256,128]{3,2,1,0:T(8,128)(2,1)S(1)}, u32[]{:S(2)}, u32[]{:S(2)}) collective-permute-start(bf16[2,2,256,128]{3,2,1,0:T(8,128)(2,1)S(1)} %bitcast.20), channel_id=1, source_target_pairs={{0,1},{1,2},{2,3},{3,4},{4,5},{5,6},{6,7},{7,8},{8,9},{9,10},{10,1... | collective-permute-start | bytes 786440 | tf_op jit(solution)/shard_map/ppermute | solution.py:23
  76.4 0.0 collective-permute-done.1.refs_2_
  76.4 1.9 %collective-permute-start.2 = (bf16[2,2,256,128]{3,2,1,0:T(8,128)(2,1)S(1)}, bf16[2,2,256,128]{3,2,1,0:T(8,128)(2,1)S(1)}, u32[]{:S(2)}, u32[]{:S(2)}) collective-permute-start(bf16[2,2,256,128]{3,2,1,0:T(8,128)(2,1)S(1)} %collective-permute-done.1.refs_2_), channel_id=1, source_target_pairs={{0,1},{1,2},{2,3},{3,4},{4,5},{5,6},{6,7},{7,8},{8,9},{9,10},{10,1... | collective-permute-start | bytes 786440 | tf_op jit(solution)/shard_map/ppermute | solution.py:23
  78.4 0.0 collective-permute-done.3.refs_3_
  78.4 4.6 %collective-permute-start.4 = (bf16[2,2,256,128]{3,2,1,0:T(8,128)(2,1)S(1)}, bf16[2,2,256,128]{3,2,1,0:T(8,128)(2,1)S(1)}, u32[]{:S(2)}, u32[]{:S(2)}) collective-permute-start(bf16[2,2,256,128]{3,2,1,0:T(8,128)(2,1)S(1)} %collective-permute-done.3.refs_3_), channel_id=1, source_target_pairs={{0,15},{1,0},{2,1},{3,2},{4,3},{5,4},{6,5},{7,6},{8,7},{9,8},{10,9... | collective-permute-start | bytes 786440 | tf_op jit(solution)/shard_map/ppermute | solution.py:23
  82.9 0.0 collective-permute-done.6.refs_4_
  83.0 1.6 %collective-permute-done.7.refs_5_ = bf16[2,2,256,128]{3,2,1,0:T(8,128)(2,1)S(1)} collective-permute-done((bf16[2,2,256,128]{3,2,1,0:T(8,128)(2,1)S(1)}, bf16[2,2,256,128]{3,2,1,0:T(8,128)(2,1)S(1)}, u32[]{:S(2)}, u32[]{:S(2)}) %collective-permute-start.7) | collective-permute-done | bytes 262176 | tf_op jit(solution)/shard_map/ppermute | solution.py:23
  84.6 0.0 collective-permute-done.5.refs_7_.refs_4_
  84.6 0.0 copy-done
  84.6 2.6 %shard_map.60 = (f32[8,2,128,128]{3,2,1,0:T(8,128)S(1)}, bf16[8,2,128,128]{3,2,1,0:T(8,128)(2,1)}, f32[8,2,128,128]{3,2,1,0:T(8,128)}) custom-call(s32[35]{0:T(128)S(1)} %pad_add_fusion.refs_0_, bf16[4,2,256,128]{3,2,1,0:T(8,128)(2,1)S(1)} %bitcast.14, bf16[2,2,256,128]{3,2,1,0:T(8,128)(2,1)S(1)} %collective-permute-done.1.refs_2_, ...), custom_call_target="tpu_custom_call" | custom-call | flops 200000000 | bytes 4000000 | tf_op jit(solution)/shard_map/pallas_call | solution.py:177
  87.2 3.0 %collective-permute-done.2.refs_1_ = bf16[2,2,256,128]{3,2,1,0:T(8,128)(2,1)S(1)} collective-permute-done((bf16[2,2,256,128]{3,2,1,0:T(8,128)(2,1)S(1)}, bf16[2,2,256,128]{3,2,1,0:T(8,128)(2,1)S(1)}, u32[]{:S(2)}, u32[]{:S(2)}) %collective-permute-start.2) | collective-permute-done | bytes 262176 | tf_op jit(solution)/shard_map/ppermute | solution.py:23
  90.2 0.0 collective-permute-done.4.refs_2_
  90.2 1.8 %shard_map.61 = (f32[8,2,128,128]{3,2,1,0:T(8,128)S(1)}, bf16[8,2,128,128]{3,2,1,0:T(8,128)(2,1)}, f32[8,2,128,128]{3,2,1,0:T(8,128)}) custom-call(s32[35]{0:T(128)S(1)} %pad_add_fusion.refs_0_, bf16[2,2,256,128]{3,2,1,0:T(8,128)(2,1)S(1)} %collective-permute-done.2.refs_1_, ...), custom_call_target="tpu_custom_call", output_to_operand_aliasing={{0}: (6, {}), {1}: (7, {}), {2}: (8, {})} | custom-call | flops 70000000 | bytes 2000000 | tf_op jit(solution)/shard_map/pallas_call | solution.py:186
  (2 shorter events, 0.1 us)
Async XLA Ops:
  0.6 12.4 %collective-permute-start = (bf16[256,128]{1,0:T(8,128)(2,1)}, bf16[256,128]{1,0:T(8,128)(2,1)S(1)}, u32[]{:S(2)}, u32[]{:S(2)}) collective-permute-start(bf16[256,128]{1,0:T(8,128)(2,1)} %bitcast.24), channel_id=1, source_target_pairs={{0,16},{1,17},{2,18},{3,19},{4,20},{5,21},{6,22},{7,23},{8,24},{9,... | collective-permute-start | bytes 196616 | tf_op jit(solution)/shard_map/ppermute | solution.py:121
  12.3 0.7 copy-start.2
  13.0 5.9 %copy-start.1 = (bf16[1,1,1,2,128,128]{5,4,3,2,1,0:T(8,128)(2,1)S(1)}, bf16[1,1,1,2,128,128]{5,4,3,2,1,0:T(8,128)(2,1)}, u32[]{:S(2)}) copy-start(bf16[1,1,1,2,128,128]{5,4,3,2,1,0:T(8,128)(2,1)} %param.4) | copy-start | bytes 196612
  13.0 38.4 %all-to-all-start = ((bf16[16,128,256]{2,1,0:T(8,128)(2,1)}), bf16[16,128,256]{2,1,0:T(8,128)(2,1)S(1)}, u32[]{:S(2)}, u32[]{:S(2)}) async-start(bf16[16,128,256]{2,1,0:T(8,128)(2,1)} %shard_map.59), calls=%async_computation | async-start | bytes 2097152 | tf_op jit(solution)/shard_map/all_to_all | solution.py:140
  18.9 65.7 %copy-start = (f32[1,1,8,2,128,128]{5,4,3,2,1,0:T(8,128)S(1)}, f32[1,1,8,2,128,128]{5,4,3,2,1,0:T(8,128)}, u32[]{:S(2)}) copy-start(f32[1,1,8,2,128,128]{5,4,3,2,1,0:T(8,128)} %param.7) | copy-start | bytes 3145732
  51.4 33.1 %collective-permute-start.5 = (bf16[16,128,256]{2,1,0:T(8,128)(2,1)S(1)}, bf16[16,128,256]{2,1,0:T(8,128)(2,1)S(1)}, u32[]{:S(2)}, u32[]{:S(2)}) collective-permute-start(bf16[16,128,256]{2,1,0:T(8,128)(2,1)S(1)} %all-to-all-done.refs_6_.refs_3_), channel_id=1, source_target_pairs={{0,32},{32,0},{64,96},{96,64},{128,160},{160,128},{192,224},{224,1... | collective-permute-start | bytes 3145736 | tf_op jit(solution)/shard_map/ppermute | solution.py:154
  58.2 18.2 %collective-permute-start.1 = (bf16[2,2,256,128]{3,2,1,0:T(8,128)(2,1)S(1)}, bf16[2,2,256,128]{3,2,1,0:T(8,128)(2,1)S(1)}, u32[]{:S(2)}, u32[]{:S(2)}) collective-permute-start(bf16[2,2,256,128]{3,2,1,0:T(8,128)(2,1)S(1)} %bitcast.21), channel_id=1, source_target_pairs={{0,1},{1,2},{2,3},{3,4},{4,5},{5,6},{6,7},{7,8},{8,9},{9,10},{10,1... | collective-permute-start | bytes 786440 | tf_op jit(solution)/shard_map/ppermute | solution.py:23
  61.5 16.8 %collective-permute-start.3 = (bf16[2,2,256,128]{3,2,1,0:T(8,128)(2,1)S(1)}, bf16[2,2,256,128]{3,2,1,0:T(8,128)(2,1)S(1)}, u32[]{:S(2)}, u32[]{:S(2)}) collective-permute-start(bf16[2,2,256,128]{3,2,1,0:T(8,128)(2,1)S(1)} %bitcast.19), channel_id=1, source_target_pairs={{0,15},{1,0},{2,1},{3,2},{4,3},{5,4},{6,5},{7,6},{8,7},{9,8},{10,9... | collective-permute-start | bytes 786440 | tf_op jit(solution)/shard_map/ppermute | solution.py:23
  71.1 11.8 %collective-permute-start.6 = (bf16[2,2,256,128]{3,2,1,0:T(8,128)(2,1)S(1)}, bf16[2,2,256,128]{3,2,1,0:T(8,128)(2,1)S(1)}, u32[]{:S(2)}, u32[]{:S(2)}) collective-permute-start(bf16[2,2,256,128]{3,2,1,0:T(8,128)(2,1)S(1)} %bitcast.22), channel_id=1, source_target_pairs={{0,15},{1,0},{2,1},{3,2},{4,3},{5,4},{6,5},{7,6},{8,7},{9,8},{10,9... | collective-permute-start | bytes 786440 | tf_op jit(solution)/shard_map/ppermute | solution.py:23
  74.5 10.1 %collective-permute-start.7 = (bf16[2,2,256,128]{3,2,1,0:T(8,128)(2,1)S(1)}, bf16[2,2,256,128]{3,2,1,0:T(8,128)(2,1)S(1)}, u32[]{:S(2)}, u32[]{:S(2)}) collective-permute-start(bf16[2,2,256,128]{3,2,1,0:T(8,128)(2,1)S(1)} %bitcast.20), channel_id=1, source_target_pairs={{0,1},{1,2},{2,3},{3,4},{4,5},{5,6},{6,7},{7,8},{8,9},{9,10},{10,1... | collective-permute-start | bytes 786440 | tf_op jit(solution)/shard_map/ppermute | solution.py:23
  76.4 13.7 %collective-permute-start.2 = (bf16[2,2,256,128]{3,2,1,0:T(8,128)(2,1)S(1)}, bf16[2,2,256,128]{3,2,1,0:T(8,128)(2,1)S(1)}, u32[]{:S(2)}, u32[]{:S(2)}) collective-permute-start(bf16[2,2,256,128]{3,2,1,0:T(8,128)(2,1)S(1)} %collective-permute-done.1.refs_2_), channel_id=1, source_target_pairs={{0,1},{1,2},{2,3},{3,4},{4,5},{5,6},{6,7},{7,8},{8,9},{9,10},{10,1... | collective-permute-start | bytes 786440 | tf_op jit(solution)/shard_map/ppermute | solution.py:23
  78.4 11.8 %collective-permute-start.4 = (bf16[2,2,256,128]{3,2,1,0:T(8,128)(2,1)S(1)}, bf16[2,2,256,128]{3,2,1,0:T(8,128)(2,1)S(1)}, u32[]{:S(2)}, u32[]{:S(2)}) collective-permute-start(bf16[2,2,256,128]{3,2,1,0:T(8,128)(2,1)S(1)} %collective-permute-done.3.refs_3_), channel_id=1, source_target_pairs={{0,15},{1,0},{2,1},{3,2},{4,3},{5,4},{6,5},{7,6},{8,7},{9,8},{10,9... | collective-permute-start | bytes 786440 | tf_op jit(solution)/shard_map/ppermute | solution.py:23
